TPU v7x, 32 devices: a whole 2x2x4 slice. The times are simulated.
32 devices in a mesh: dp: 8 (over z, y), seq: 4 (over x, core).
Axes of the slice: x: 2, y: 2, z: 4, core: 2. Of those that a mesh axis runs over, the one named last changes fastest.
Arguments:
- tokens: bfloat16 [16, 512, 768], P('dp', 'seq'), may hold values from -6 to 6
- lengths: int32 [8, 2], P('dp'), may hold values from 1 to 512, 640 in all within a row
- cotangent: bfloat16 [16, 512, 768], P('dp', 'seq'), may hold values from -6 to 6
- w_qkv: bfloat16 [768, 2304], replicated, may hold values from -0.21875 to 0.21875
- b_query: float32 [768], replicated, may hold values from -4 to 4
- b_value: float32 [768], replicated, may hold values from -3 to 3
- w_out: bfloat16 [768, 768], replicated, may hold values from -1.75 to 1.75
- b_out: float32 [768], replicated, may hold values from -3 to 3
- first_gain: float32 [768], replicated, may hold values from 0.5 to 1.5
- first_shift: float32 [768], replicated, may hold values from -3 to 3
- w_up: bfloat16 [768, 3072], replicated, may hold values from -0.21875 to 0.21875
- b_up: float32 [3072], replicated, may hold values from -3 to 3
- w_down: bfloat16 [3072, 768], replicated, may hold values from -0.109375 to 0.109375
- b_down: float32 [768], replicated, may hold values from -3 to 3
- second_gain: float32 [768], replicated, may hold values from 0.5 to 1.5
- second_shift: float32 [768], replicated, may hold values from -3 to 3
Outputs:
- output_tokens: bfloat16 [16, 512, 768], P('dp', 'seq')
- grad_tokens: bfloat16 [16, 512, 768], P('dp', 'seq')
- grad_w_qkv: float32 [768, 2304], P('dp', 'seq')
- grad_w_out: float32 [768, 768], P('dp', 'seq')
- grad_w_up: float32 [768, 3072], P('dp', 'seq')
- grad_w_down: float32 [3072, 768], P('dp', 'seq')
- grad_b_query: float32 [768], replicated
- grad_b_value: float32 [768], replicated
- grad_b_out: float32 [768], replicated
- grad_first_gain: float32 [768], replicated
- grad_first_shift: float32 [768], replicated
- grad_b_up: float32 [3072], replicated
- grad_b_down: float32 [768], replicated
- grad_second_gain: float32 [768], replicated
- grad_second_shift: float32 [768], replicated
Inputs may be any that keep to these rules, and one draw needn't show every extreme that they name: In each row of lengths the 2 lengths sum to 640.
All inputs are finite; a program needn't handle non-finite values.
Results may differ from a plain program's by a relative error of at most 0.015.
Values may be sent and summed in bfloat16 or wider, within the bound.
A program may use at most 128 MiB of HBM per device.

v0:
```python
import jax
import jax.numpy as jnp
from jax import lax
from jax.sharding import PartitionSpec as P

HEAD_DIM = 64


EPSILON = 1e-05
ROOT_HALF = 0.7071067811865476
INV_ROOT_TWO_PI = 0.3989422804014327


def contract_rows(left, right):
    return lax.dot_general(
        left, right, (((0,), (0,)), ((), ())), preferred_element_type=jnp.float32
    )


def times_transposed(left, weight_matrix):
    return lax.dot_general(
        left, weight_matrix, (((1,), (1,)), ((), ())), preferred_element_type=jnp.float32
    )


def normalize(value_rows):
    center = value_rows - jnp.mean(value_rows, axis=-1, keepdims=True)
    inverse_root = lax.rsqrt(jnp.mean(center * center, axis=-1, keepdims=True) + EPSILON)
    return (center * inverse_root, inverse_root)


def norm_backward(grad_out, normed, inverse_root, gain):
    scaled = grad_out * gain
    return inverse_root * (
        scaled
        - jnp.mean(scaled, axis=-1, keepdims=True)
        - normed * jnp.mean(scaled * normed, axis=-1, keepdims=True)
    )


def attention_forward_pass(inputs):
    queries, key_block, value_block, key_valid = inputs
    head_scale = queries.shape[-1] ** (-0.5)
    scores = (
        jnp.einsum("qhd,khd->hqk", queries, key_block, preferred_element_type=jnp.float32)
        * head_scale
    )
    scores = jnp.where(key_valid[None, None, :], scores, -1e30)
    highest = jnp.max(scores, axis=-1, keepdims=True)
    exponent = jnp.exp(scores - highest)
    row_total = jnp.sum(exponent, axis=-1, keepdims=True)
    weight_tensors = (exponent / row_total).astype(jnp.bfloat16)
    context = jnp.einsum(
        "hqk,khd->qhd", weight_tensors, value_block, preferred_element_type=jnp.float32
    )
    return (context.astype(jnp.bfloat16), (highest + jnp.log(row_total))[..., 0])


def attend_backward(inputs):
    queries, key_block, value_block, key_valid, log_total, grad_context = inputs
    head_scale = queries.shape[-1] ** (-0.5)
    scores = (
        jnp.einsum("qhd,khd->hqk", queries, key_block, preferred_element_type=jnp.float32)
        * head_scale
    )
    scores = jnp.where(key_valid[None, None, :], scores, -1e30)
    probs = jnp.exp(scores - log_total[..., None])
    grad_probs = jnp.einsum(
        "qhd,khd->hqk", grad_context, value_block, preferred_element_type=jnp.float32
    )
    row_inner = jnp.sum(probs * grad_probs, axis=-1, keepdims=True)
    grad_scores = (probs * (grad_probs - row_inner)).astype(jnp.bfloat16)
    probs_low = probs.astype(jnp.bfloat16)
    grad_queries = (
        jnp.einsum("hqk,khd->qhd", grad_scores, key_block, preferred_element_type=jnp.float32)
        * head_scale
    )
    grad_keys = (
        jnp.einsum("hqk,qhd->khd", grad_scores, queries, preferred_element_type=jnp.float32)
        * head_scale
    )
    grad_values = jnp.einsum(
        "hqk,qhd->khd", probs_low, grad_context, preferred_element_type=jnp.float32
    )
    return jnp.stack([grad_queries, grad_keys, grad_values], axis=1).astype(jnp.bfloat16)


def local(
    tokens,
    lengths,
    cotangent,
    w_qkv,
    b_query,
    b_value,
    w_out,
    b_out,
    first_gain,
    first_shift,
    w_up,
    b_up,
    w_down,
    b_down,
    second_gain,
    second_shift,
):
    lane_count = lax.axis_size("seq")
    seq_count, part_len, model_width = tokens.shape
    full_len = part_len * lane_count
    lane_width = model_width // lane_count
    head_size = HEAD_DIM
    heads_here = lane_width // head_size
    row_count = seq_count * part_len
    offset = lax.axis_index("seq") * part_len
    places = offset + jnp.arange(part_len, dtype=jnp.int32)
    length_row = lengths[0]
    row_live = (places[None, :] < length_row[:, None]).astype(jnp.float32).reshape(row_count, 1)
    key_valid = jnp.arange(full_len, dtype=jnp.int32)[None, :] < length_row[:, None]
    joined_bias = jnp.concatenate([b_query, jnp.zeros_like(b_query), b_value])
    tokens_flat = tokens.reshape(row_count, model_width)
    mixed = jnp.dot(tokens_flat, w_qkv, preferred_element_type=jnp.float32) + joined_bias
    qkv_heads = lax.all_to_all(
        mixed.astype(jnp.bfloat16).reshape(seq_count, part_len, 3, lane_count, lane_width),
        "seq",
        split_axis=3,
        concat_axis=1,
        tiled=True,
    )
    qkv_heads = qkv_heads.reshape(seq_count, full_len, 3, heads_here, head_size)
    context_heads, log_total = lax.map(
        attention_forward_pass,
        (qkv_heads[:, :, 0], qkv_heads[:, :, 1], qkv_heads[:, :, 2], key_valid),
    )
    context_heads = context_heads.reshape(seq_count, full_len, 1, lane_width)
    context_token_rows = lax.all_to_all(
        context_heads, "seq", split_axis=1, concat_axis=2, tiled=True
    ).reshape(row_count, model_width)
    branch = jnp.dot(context_token_rows, w_out, preferred_element_type=jnp.float32) + b_out
    normed_one, inverse_one = normalize(tokens_flat.astype(jnp.float32) + branch)
    hidden = normed_one * first_gain + first_shift
    hidden_low = hidden.astype(jnp.bfloat16)
    preactivation_input = jnp.dot(hidden_low, w_up, preferred_element_type=jnp.float32) + b_up
    active = jax.nn.gelu(preactivation_input, approximate=False).astype(jnp.bfloat16)
    ffn_out = jnp.dot(active, w_down, preferred_element_type=jnp.float32) + b_down
    normed_two, inverse_two = normalize(hidden + ffn_out)
    output_rows = (normed_two * second_gain + second_shift) * row_live
    output_tokens = output_rows.astype(jnp.bfloat16).reshape(seq_count, part_len, model_width)
    grad_out = cotangent.reshape(row_count, model_width).astype(jnp.float32) * row_live
    grad_second_gain = jnp.sum(grad_out * normed_two, axis=0)
    grad_second_shift = jnp.sum(grad_out, axis=0)
    d_sum_two = norm_backward(grad_out, normed_two, inverse_two, second_gain)
    d_ffn = d_sum_two.astype(jnp.bfloat16)
    grad_b_down = jnp.sum(d_ffn.astype(jnp.float32), axis=0)
    grad_w_down = contract_rows(active, d_ffn)
    d_active = times_transposed(d_ffn, w_down)
    gelu_slope = (
        0.5 * (1.0 + lax.erf(preactivation_input * ROOT_HALF))
        + preactivation_input
        * jnp.exp(-0.5 * preactivation_input * preactivation_input)
        * INV_ROOT_TWO_PI
    )
    d_pre = (d_active * gelu_slope).astype(jnp.bfloat16)
    grad_b_up = jnp.sum(d_pre.astype(jnp.float32), axis=0)
    grad_w_up = contract_rows(hidden_low, d_pre)
    d_hidden = d_sum_two + times_transposed(d_pre, w_up)
    grad_first_gain = jnp.sum(d_hidden * normed_one, axis=0)
    grad_first_shift = jnp.sum(d_hidden, axis=0)
    d_sum_one = norm_backward(d_hidden, normed_one, inverse_one, first_gain)
    d_branch = d_sum_one.astype(jnp.bfloat16)
    grad_b_out = jnp.sum(d_branch.astype(jnp.float32), axis=0)
    grad_w_out = contract_rows(context_token_rows, d_branch)
    d_context = times_transposed(d_branch, w_out).astype(jnp.bfloat16)
    d_context = d_context.reshape(seq_count, part_len, lane_count, lane_width)
    d_context_heads = lax.all_to_all(d_context, "seq", split_axis=2, concat_axis=1, tiled=True)
    d_context_heads = d_context_heads.reshape(seq_count, full_len, heads_here, head_size)
    d_qkv_heads = lax.map(
        attend_backward,
        (
            qkv_heads[:, :, 0],
            qkv_heads[:, :, 1],
            qkv_heads[:, :, 2],
            key_valid,
            log_total,
            d_context_heads,
        ),
    )
    d_qkv_heads = d_qkv_heads.reshape(seq_count, full_len, 3, 1, lane_width)
    d_qkv = lax.all_to_all(d_qkv_heads, "seq", split_axis=1, concat_axis=3, tiled=True).reshape(
        row_count, 3 * model_width
    )
    d_qkv_wide = d_qkv.astype(jnp.float32)
    grad_b_query = jnp.sum(d_qkv_wide[:, :model_width], axis=0)
    grad_b_value = jnp.sum(d_qkv_wide[:, 2 * model_width :], axis=0)
    grad_w_qkv = contract_rows(tokens_flat, d_qkv)
    grad_rows = d_sum_one + times_transposed(d_qkv, w_qkv)
    grad_tokens = grad_rows.astype(jnp.bfloat16).reshape(seq_count, part_len, model_width)
    matrices = (grad_w_qkv, grad_w_out, grad_w_up, grad_w_down)
    halfway = (
        lax.psum_scatter(matrices[0], "dp", scatter_dimension=0, tiled=True),
        lax.psum_scatter(matrices[1], "dp", scatter_dimension=0, tiled=True),
        lax.psum_scatter(matrices[2], "dp", scatter_dimension=0, tiled=True),
        lax.psum_scatter(matrices[3], "dp", scatter_dimension=0, tiled=True),
    )
    matrices = (
        lax.psum_scatter(
            halfway[0].astype(jnp.bfloat16), "seq", scatter_dimension=1, tiled=True
        ).astype(jnp.float32),
        lax.psum_scatter(
            halfway[1].astype(jnp.bfloat16), "seq", scatter_dimension=1, tiled=True
        ).astype(jnp.float32),
        lax.psum_scatter(
            halfway[2].astype(jnp.bfloat16), "seq", scatter_dimension=1, tiled=True
        ).astype(jnp.float32),
        lax.psum_scatter(
            halfway[3].astype(jnp.bfloat16), "seq", scatter_dimension=1, tiled=True
        ).astype(jnp.float32),
    )
    vectors = lax.psum(
        (
            grad_b_query,
            grad_b_value,
            grad_b_out,
            grad_first_gain,
            grad_first_shift,
            grad_b_up,
            grad_b_down,
            grad_second_gain,
            grad_second_shift,
        ),
        ("dp", "seq"),
    )
    return (
        output_tokens,
        grad_tokens,
        matrices[0],
        matrices[1],
        matrices[2],
        matrices[3],
        vectors[0],
        vectors[1],
        vectors[2],
        vectors[3],
        vectors[4],
        vectors[5],
        vectors[6],
        vectors[7],
        vectors[8],
    )


def solution(mesh):
    in_specs = (
        P("dp", "seq", None),
        P("dp", None),
        P("dp", "seq", None),
        P(),
        P(),
        P(),
        P(),
        P(),
        P(),
        P(),
        P(),
        P(),
        P(),
        P(),
        P(),
        P(),
    )
    out_specs = (
        P("dp", "seq", None),
        P("dp", "seq", None),
        P("dp", "seq"),
        P("dp", "seq"),
        P("dp", "seq"),
        P("dp", "seq"),
        P(),
        P(),
        P(),
        P(),
        P(),
        P(),
        P(),
        P(),
        P(),
    )
    return jax.shard_map(local, mesh=mesh, in_specs=in_specs, out_specs=out_specs, check_vma=False)
```

profile of v0, /device:TPU:0, one launch (start us, length us, event | category | flops | bytes accessed | tf_op | source)
XLA Modules:
  0.0 757.6 jit_solution(13337180512320921938)
XLA Ops:
  9.2 3.1 fusion.50
  12.3 4.4 reshape.252
  16.7 5.2 copy.98
  21.9 4.3 all-to-all-start
  26.9 15.8 %all-to-all-done = bf16[2,128,3,4,192]{1,0,4,2,3:T(2,128)(2,1)} async-done(((bf16[2,128,3,4,192]{1,0,4,2,3:T(2,128)(2,1)}), bf16[2,128,3,4,192]{1,0,4,2,3:T(2,128)(2,1)}, u32[]{:S(2)}, u32[]{:S(2)}) %all-to-all-start) | async-done | bytes 1179680 | tf_op jit(solution)/shard_map/all_to_all | solution.py:121
  42.7 3.2 copy.99
  45.9 3.2 reshape.241
  49.2 2.3 slice_bitcast_fusion
  51.5 9.6 %while.22 = (s32[]{:T(128)}, bf16[2,512,3,64]{1,3,2,0:T(8,128)(2,1)}, f32[2,3,512]{2,1,0:T(4,128)}, bf16[2,512,3,64]{1,3,2,0:T(8,128)(2,1)}, pred[2,512]{1,0:T(4...) while((s32[]{:T(128)}, ...), condition=%wide.region_3.4_spmd, body=%wide.region_0.3_spmd.sunk | while | flops 210860544 | bytes 11857013 | solution.py:129
  63.1 4.3 all-to-all-start.1
  70.6 5.6 all-to-all-done.1
  82.2 9.7 %fusion.53 = (bf16[256,3072]{1,0:T(8,128)(2,1)S(1)}, f32[256,3072]{1,0:T(8,128)S(1)}) fusion(f32[3072]{0:T(1024)S(1)} %copy-done.27, bf16[768,3072]{1,0:T(8,128)(2,1)} %param.30, f32[256,768]{1,0:T(8,128)S(1)} %get-tuple-element.252, f32[768]{0:T(1024)S(1)} %copy-done.15, f32[768]{0:T(1024)S(1)} %copy-done.14, f32[256]{0:T(256)S(1)} %add_rsqrt_fusion.1, ...), kind=kOutput, calls=%fused_computation.68 | convolution fusion | flops 1260847104 | bytes 10244096 | tf_op jit(solution)/shard_map/dot_general | solution.py:141
  96.6 3.0 convert_reduce_fusion
  108.1 4.1 all-to-all-start.2
  112.3 3.2 fusion.75
  115.7 4.0 all-to-all-done.2
  123.6 13.8 %while.23 = (s32[]{:T(128)}, bf16[2,512,3,3,64]{1,4,3,2,0:T(8,128)(2,1)}, bf16[2,512,3,64]{1,3,2,0:T(8,128)(2,1)}, pred[2,512]{1,0:T(4,128)(4,1)S(1)}, bf16[2,51...) while((s32[]{:T(128)}, ...), condition=%wide.region_14.15_spmd, body=%wide.region_12.14_spmd.sunk | while | flops 512653824 | bytes 31494340 | solution.py:175
  137.4 4.9 copy.105
  142.3 24.5 %all_to_all.60 = bf16[2,512,3,1,192]{4,0,3,2,1:T(2,128)(2,1)} all-to-all(bf16[2,512,3,1,192]{4,0,3,2,1:T(2,128)(2,1)} %copy.105), channel_id=1, replica_groups=mesh['dp'=8,'seq'=4] {'seq'}, dimensions={1} | all-to-all | bytes 2359296 | tf_op jit(solution)/shard_map/all_to_all | solution.py:187
  166.8 5.1 copy.117
  171.9 2.5 copy.107
  175.4 5.0 convolution_bitcast_fusion
  180.4 8.0 %copy.118 = f32[768,2304]{1,0:T(8,128)} copy(f32[768,2304]{0,1:T(8,128)} %convolution_bitcast_fusion) | data formatting | bytes 14155776
  188.5 6.7 fusion.82
  195.9 6.9 fusion.86
  206.3 113.8 %reduce-scatter.25.cloned.1.call-done = f32[96,2304]{1,0:T(8,128)} async-done(((f32[768,2304]{1,0:T(8,128)}), f32[96,2304]{1,0:T(8,128)}) %reduce-scatter.25.cloned.1.call-update) | async-done | bytes 884752
  322.4 164.3 %reduce-scatter.23.cloned.1.call-done = f32[384,768]{1,0:T(8,128)} async-done(((f32[3072,768]{1,0:T(8,128)}), f32[384,768]{1,0:T(8,128)}) %reduce-scatter.23.cloned.1.call-update) | async-done | bytes 1179664 | tf_op jit(solution)/shard_map/reduce_scatter | solution.py:201
  491.0 162.0 %reduce-scatter.19.cloned.1.call-done = f32[96,3072]{1,0:T(8,128)} async-done(((f32[768,3072]{1,0:T(8,128)}), f32[96,3072]{1,0:T(8,128)}) %reduce-scatter.19.cloned.1.call-update) | async-done | bytes 1179664 | tf_op jit(solution)/shard_map/reduce_scatter | solution.py:200
  657.5 41.1 %all-reduce = (f32[768]{0:T(1024)}, f32[768]{0:T(1024)}, f32[768]{0:T(1024)}, f32[768]{0:T(1024)}, f32[768]{0:T(1024)}, /*index=5*/f32[3072]{0:T(1024)}, f32[768]{0:T(1024)}, f32[768]{0:T(1024)}, f32[768]{0:T(1024)}) all-reduce(f32[768]{0:T(1024)} %get-tuple-element.189, ...), channel_id=1, replica_groups=mesh['dp'=8,'seq'=4] {'dp','seq'}, use_global_device_ids=true, to_apply=%region_24.25 | all-reduce | flops 9216 | bytes 73728 | tf_op jit(solution)/shard_map/psum | solution.py:217
  698.6 3.4 fusion.67
  706.7 17.7 %reduce-scatter.29.cloned.1.call-done = bf16[192,384]{1,0:T(8,128)(2,1)} async-done(((bf16[768,384]{1,0:T(8,128)(2,1)}), bf16[192,384]{1,0:T(8,128)(2,1)}) %reduce-scatter.29.cloned.1.call-update) | async-done | bytes 147472
  727.9 21.3 %reduce-scatter.21.cloned.1.call-done = bf16[96,768]{1,0:T(8,128)(2,1)} async-done(((bf16[96,3072]{1,0:T(8,128)(2,1)}), bf16[96,768]{1,0:T(8,128)(2,1)}) %reduce-scatter.21.cloned.1.call-update) | async-done | bytes 147472 | tf_op jit(solution)/shard_map/reduce_scatter | solution.py:210
  (169 shorter events, 80.5 us)
Async XLA Ops:
  16.7 9.5 %copy-start.26 = (s32[1,2]{1,0:T(1,128)S(1)}, s32[1,2]{1,0:T(1,128)}, u32[]{:S(2)}) copy-start(s32[1,2]{1,0:T(1,128)} %param.21) | copy-start | bytes 28
  21.9 20.8 %all-to-all-start = ((bf16[2,128,3,4,192]{1,0,4,2,3:T(2,128)(2,1)}), bf16[2,128,3,4,192]{1,0,4,2,3:T(2,128)(2,1)}, u32[]{:S(2)}, u32[]{:S(2)}) async-start(bf16[2,128,3,4,192]{1,0,4,2,3:T(2,128)(2,1)} %copy.98), calls=%async_computation | async-start | bytes 2359296 | tf_op jit(solution)/shard_map/all_to_all | solution.py:121
  51.5 16.0 %copy-start.16 = (f32[768]{0:T(1024)S(1)}, f32[768]{0:T(1024)}, u32[]{:S(2)}) copy-start(f32[768]{0:T(1024)} %param.34) | copy-start | bytes 9220
  51.5 3.2 copy-start.7
  56.4 3.2 copy-start.7
  63.1 13.0 %all-to-all-start.1 = ((bf16[2,512,1,192]{3,0,2,1:T(2,128)(2,1)}), bf16[2,512,1,192]{3,0,2,1:T(2,128)(2,1)}, u32[]{:S(2)}, u32[]{:S(2)}) async-start(bf16[2,512,1,192]{3,0,2,1:T(2,128)(2,1)} %copy.100), calls=%async_computation.1 | async-start | bytes 1048576 | tf_op jit(solution)/shard_map/all_to_all | solution.py:134
  67.4 14.7 %copy-start.14 = (f32[768]{0:T(1024)S(1)}, f32[768]{0:T(1024)}, u32[]{:S(2)}) copy-start(f32[768]{0:T(1024)} %param.28) | copy-start | bytes 9220
  67.5 14.7 %copy-start.15 = (f32[768]{0:T(1024)S(1)}, f32[768]{0:T(1024)}, u32[]{:S(2)}) copy-start(f32[768]{0:T(1024)} %param.29) | copy-start | bytes 9220
  78.3 3.9 copy-start.27
  79.7 12.3 %slice-start = ((s8[4718592]{0:T(1024)(128)(4,1)}), s8[4194304]{0:T(1024)(128)(4,1)S(1)}, s32[]{:S(2)}) async-start(s8[4718592]{0:T(1024)(128)(4,1)} %bitcast.198), calls=%async_computation.20 | async-start | bytes 8388608
  81.9 20.0 %copy-start.6 = (f32[256,768]{1,0:T(8,128)}, f32[256,768]{1,0:T(8,128)S(1)}, u32[]{:S(2)}) copy-start(f32[256,768]{1,0:T(8,128)S(1)} %get-tuple-element.252) | copy-start | bytes 2359300
  81.9 20.0 %copy-start.17 = (f32[256]{0:T(256)}, f32[256]{0:T(256)S(1)}, u32[]{:S(2)}) copy-start(f32[256]{0:T(256)S(1)} %broadcast_multiply_fusion.4) | copy-start | bytes 3076
  82.2 19.7 %copy-start.22 = (f32[256]{0:T(256)}, f32[256]{0:T(256)S(1)}, u32[]{:S(2)}) copy-start(f32[256]{0:T(256)S(1)} %add_rsqrt_fusion.1) | copy-start | bytes 3076
  82.2 9.8 %slice-start.1 = ((s8[4718592]{0:T(1024)(128)(4,1)}), s8[524288]{0:T(1024)(128)(4,1)S(1)}, s32[]{:S(2)}) async-start(s8[4718592]{0:T(1024)(128)(4,1)} %bitcast.198), calls=%async_computation.21 | async-start | bytes 1048576
  82.2 9.8 %copy-start.28 = (f32[768]{0:T(1024)S(1)}, f32[768]{0:T(1024)}, u32[]{:S(2)}) copy-start(f32[768]{0:T(1024)} %param.33) | copy-start | bytes 9220
  92.0 2.8 copy-start.24
  92.1 2.8 copy-start.25
  93.9 5.7 slice-start.2
  96.6 3.0 copy-start.9
  96.6 3.0 slice-start.3
  99.6 3.5 copy-start.13
  108.1 11.6 %all-to-all-start.2 = ((bf16[2,128,4,192]{1,0,3,2:T(2,128)(2,1)}), bf16[2,128,4,192]{1,0,3,2:T(2,128)(2,1)}, u32[]{:S(2)}, u32[]{:S(2)}) async-start(bf16[2,128,4,192]{1,0,3,2:T(2,128)(2,1)} %reshape.245), calls=%async_computation.2 | async-start | bytes 786432 | tf_op jit(solution)/shard_map/all_to_all | solution.py:173
  112.2 90.7 %reduce-scatter.17.cloned.1.call-start = ((), (), s32[]{:S(2)}) async-start(), calls=%async_computation.13 | async-start | bytes 2654208 | tf_op jit(solution)/shard_map/reduce_scatter | solution.py:199
  115.4 204.6 %reduce-scatter.25.cloned.1.call-start = ((), (), s32[]{:S(2)}) async-start(), calls=%async_computation.17 | async-start | bytes 7962624
  130.5 2.5 copy-start.1
  130.5 2.5 copy-start.2
  188.5 298.2 %reduce-scatter.23.cloned.1.call-start = ((), (), s32[]{:S(2)}) async-start(), calls=%async_computation.16 | async-start | bytes 10616832 | tf_op jit(solution)/shard_map/reduce_scatter | solution.py:201
  195.3 457.7 %reduce-scatter.19.cloned.1.call-start = ((), (), s32[]{:S(2)}) async-start(), calls=%async_computation.14 | async-start | bytes 10616832 | tf_op jit(solution)/shard_map/reduce_scatter | solution.py:200
  202.8 499.2 %reduce-scatter.27.cloned.1.call-start = ((), (), s32[]{:S(2)}) async-start(), calls=%async_computation.18 | async-start | bytes 245760
  206.3 498.7 %reduce-scatter.15.cloned.1.call-start = ((), (), s32[]{:S(2)}) async-start(), calls=%async_computation.12 | async-start | bytes 737280 | tf_op jit(solution)/shard_map/reduce_scatter | solution.py:204
  322.3 402.0 %reduce-scatter.29.cloned.1.call-start = ((), (), s32[]{:S(2)}) async-start(), calls=%async_computation.19 | async-start | bytes 737280
  491.0 258.2 %reduce-scatter.21.cloned.1.call-start = ((), (), s32[]{:S(2)}) async-start(), calls=%async_computation.15 | async-start | bytes 737280 | tf_op jit(solution)/shard_map/reduce_scatter | solution.py:210
  (16 other events, 28.7 us)
Sparse Core Ops, SparseCore 0:
  116.5 71.7 reduce-scatter.16
  192.0 128.0 reduce-scatter.24
  324.1 162.4 reduce-scatter.22
  490.5 162.3 reduce-scatter.18
  656.0 18.8 reduce-scatter.26
  677.3 22.3 reduce-scatter.14
  702.4 21.9 reduce-scatter.28
  727.0 22.0 reduce-scatter.20
where the time goes:
time: 760 us; the launch traced here: 758 us
  waiting for transfers between devices  504 us (66%)
  local copies, waits for them, and re-layouts  70.2 us (9%)
  blocking collectives  65.6 us (9%)
  matrix products  63.9 us (8%)
  other arithmetic  25.5 us (3%)
  between operations  14.6 us (2%)
  starting transfers between devices  13.2 us (2%)
    reduce_scatter x1, waiting for transfers between devices, local(): lax.psum_scatter(matrices[3], 'dp', scatter_dimension=0, tiled=True)  164 us
    reduce_scatter x1, waiting for transfers between devices, local(): lax.psum_scatter(matrices[2], 'dp', scatter_dimension=0, tiled=True)  162 us
    unnamed x11, waiting for transfers between devices  132 us
    psum x1, blocking collectives, local(): lax.psum((grad_b_query, grad_b_value, grad_b_out, grad_first_gain, grad_f...  41.1 us
    unnamed x66, local copies, waits for them, and re-layouts  24.6 us
    all_to_all x1, blocking collectives, local(): lax.all_to_all(d_qkv_heads, 'seq', split_axis=1, concat_axis=3, tiled=True)  24.5 us
    dot_general x4, matrix products, contract_rows(): lax.dot_general(left, right, (((0,), (0,)), ((), ())), preferred_element_...  21.7 us
    reduce_scatter x1, waiting for transfers between devices, local(): lax.psum_scatter(halfway[2].astype(jnp.bfloat16), 'seq', scatter_dimensio...  21.3 us
  transfers between devices with their start and end apart: 11, of which 8 were waited for; matrix products, arithmetic and copies ran while one was open for 12% of the time, Pallas kernels for 0%

commit v1 on v0

--- a/solution.py
+++ b/solution.py
@@ -1,7 +1,15 @@
+import functools
+
 import jax
 import jax.numpy as jnp
 from jax import lax
+from jax.experimental import pallas as pl
+from jax.experimental.pallas import tpu as pltpu
 from jax.sharding import PartitionSpec as P
+
+MESH_ID = pl.DeviceIdType.MESH
+BF16 = jnp.bfloat16
+F32 = jnp.float32
 
 HEAD_DIM = 64
 
@@ -83,6 +91,404 @@
         "hqk,qhd->khd", probs_low, grad_context, preferred_element_type=jnp.float32
     )
     return jnp.stack([grad_queries, grad_keys, grad_values], axis=1).astype(jnp.bfloat16)
+
+
+DOWN, UP, QKV = 0, 1, 2
+CHUNKS = tuple((m, k) for k in (1, 2, 3, 0) for m in (DOWN, UP)) + tuple((QKV, k) for k in (1, 2, 3, 0))
+X_FIRST = {(UP, 0), (UP, 1), (UP, 2), (UP, 3), (QKV, 2), (QKV, 0)}
+
+
+def place():
+    row, lane = lax.axis_index("dp"), lax.axis_index("seq")
+    return row // 2, row % 2, lane // 2, lane % 2
+
+
+def device(z, y, x, core):
+    return (z * 2 + y, x * 2 + core)
+
+
+def remote(source, target, send, receive, where):
+    return pltpu.make_async_remote_copy(
+        src_ref=source,
+        dst_ref=target,
+        send_sem=send,
+        recv_sem=receive,
+        device_id=where,
+        device_id_type=MESH_ID,
+    )
+
+
+def grad_kernel(
+    hid_ref, dpre_ref, act_ref, dffn_ref, tok_ref, dqkv_ref, ctx_ref, dbr_ref, vec_ref,
+    down_out, up_out, qkv_out, vec_out,
+    act, dpre, dffn_t, hid_t, tok_t, ctx_t, dqkv, dbr,
+    sums_0, sums_1, sums_2, in1_0, in1_1, in1_2, in2_0, in2_1, in2_2, in3_0, in3_1, in3_2,
+    vec_mine, vec_in,
+    core_send, core_recv, send1, recv1, send2, recv2, send3, recv3, vec_send, vec_recv,
+):
+    z, y, x, core = place()
+    sums, in1, in2, in3 = (sums_0, sums_1, sums_2), (in1_0, in1_1, in1_2), (in2_0, in2_1, in2_2), (in3_0, in3_1, in3_2)
+    at_core = device(z, y, x, 1 - core)
+    at_x = device(z, y, 1 - x, core)
+    at_y = device(z, 1 - y, x, core)
+    at_z = [device((z + k) % 4, y, x, core) for k in (1, 2, 3)]
+    barrier = pltpu.get_barrier_semaphore()
+    for where in [at_core, at_x, at_y] + at_z:
+        pl.semaphore_signal(barrier, inc=1, device_id=where, device_id_type=MESH_ID)
+    pl.semaphore_wait(barrier, 6)
+
+    R = 256
+    core_copies = []
+
+    def to_core(source, target):
+        n = len(core_copies)
+        copy = remote(source, target, core_send.at[n], core_recv.at[n], at_core)
+        copy.start()
+        core_copies.append(copy)
+        return copy
+
+    act_copies = []
+    for t in range(4):
+        act[t, 0:R, :] = act_ref[:, 768 * t : 768 * (t + 1)]
+        act_copies.append(to_core(act.at[t, pl.ds(0, R)], act.at[t, pl.ds(R, R)]))
+    dffn_all = dffn_ref[...].T
+    for j in range(4):
+        dffn_t[j, :, 0:R] = dffn_all[192 * j : 192 * (j + 1), :]
+    for j in (0, 2):
+        there = j + 1 - core
+        act_copies.append(to_core(dffn_t.at[there, :, pl.ds(0, R)], dffn_t.at[there, :, pl.ds(R, R)]))
+    hid_t[:, 0:R] = hid_ref[...].T
+    up_copies = [to_core(hid_t.at[:, pl.ds(0, R)], hid_t.at[:, pl.ds(R, R)])]
+    for t in range(4):
+        dpre[t, 0:R, :] = dpre_ref[:, 768 * t : 768 * (t + 1)]
+    for j in (0, 2):
+        there = j + 1 - core
+        up_copies.append(to_core(dpre.at[there, pl.ds(0, R)], dpre.at[there, pl.ds(R, R)]))
+    tok_t[:, 0:R] = tok_ref[...].T
+    ctx_t[:, 0:R] = ctx_ref[...].T
+    qkv_copies = [
+        to_core(tok_t.at[:, pl.ds(0, R)], tok_t.at[:, pl.ds(R, R)]),
+        to_core(ctx_t.at[:, pl.ds(0, R)], ctx_t.at[:, pl.ds(R, R)]),
+    ]
+    for j in range(4):
+        dqkv[j, 0:R, :] = jnp.concatenate(
+            [dqkv_ref[:, 576 * j : 576 * (j + 1)], jnp.zeros((R, 64), BF16)], axis=1
+        )
+        dbr[j, 0:R, :] = jnp.concatenate(
+            [jnp.zeros((R, 64), BF16), dbr_ref[:, 192 * j : 192 * (j + 1)]], axis=1
+        )
+    for j in (0, 2):
+        there = j + 1 - core
+        qkv_copies.append(to_core(dqkv.at[there, pl.ds(0, R)], dqkv.at[there, pl.ds(R, R)]))
+        qkv_copies.append(to_core(dbr.at[there, pl.ds(0, R)], dbr.at[there, pl.ds(R, R)]))
+
+    def first(m, k):
+        zk = (z + k) % 4
+        if (m, k) in X_FIRST:
+            return remote(sums[m].at[1 - x, zk], in1[m].at[zk], send1.at[m, k], recv1.at[m, k], at_x)
+        return remote(sums[m].at[:, zk, 1 - y], in1[m].at[zk], send1.at[m, k], recv1.at[m, k], at_y)
+
+    def second(m, k):
+        zk = (z + k) % 4
+        if (m, k) in X_FIRST:
+            return remote(sums[m].at[x, zk, 1 - y], in2[m].at[zk], send2.at[m, k], recv2.at[m, k], at_y)
+        return remote(sums[m].at[1 - x, zk, y], in2[m].at[zk], send2.at[m, k], recv2.at[m, k], at_x)
+
+    def third(m, k):
+        zk = (z + k) % 4
+        return remote(sums[m].at[x, zk, y], in3[m].at[k - 1], send3.at[m, k], recv3.at[m, k], at_z[k - 1])
+
+    def add_first(m, k):
+        zk = (z + k) % 4
+        if (m, k) in X_FIRST:
+            sums[m][x, zk] = sums[m][x, zk] + in1[m][zk]
+        else:
+            for b in range(2):
+                sums[m][b, zk, y] = sums[m][b, zk, y] + in1[m][zk, b]
+
+    def add_second(m, k):
+        zk = (z + k) % 4
+        sums[m][x, zk, y] = sums[m][x, zk, y] + in2[m][zk]
+
+    vec_mine[0] = vec_ref[...]
+    vec_steps = [remote(vec_mine.at[s], vec_in.at[s], vec_send.at[s], vec_recv.at[s], w) for s, w in enumerate((at_core, at_x, at_y))]
+    vec_steps[0].start()
+
+    for copy in act_copies:
+        copy.wait_recv()
+    left = jnp.concatenate([dffn_t[core], dffn_t[2 + core]], axis=0)
+    for t in range(4):
+        part = jnp.dot(left, act[t], preferred_element_type=F32).astype(BF16)
+        for b in range(2):
+            for h in range(2):
+                sums_0[b, t, h] = part[192 * b : 192 * (b + 1), 384 * h : 384 * (h + 1)]
+    for k in (1, 2, 3, 0):
+        first(DOWN, k).start()
+    for copy in up_copies:
+        copy.wait_recv()
+    for b in range(2):
+        for n in range(3):
+            part = jnp.dot(hid_t[...], dpre[2 * b + core, :, 256 * n : 256 * (n + 1)], preferred_element_type=F32).astype(BF16)
+            sums_1[b, :, :, :, 256 * n : 256 * (n + 1)] = part.reshape(4, 2, 96, 256)
+    for k in (1, 2, 3, 0):
+        first(UP, k).start()
+    vec_steps[0].wait_recv()
+    vec_mine[1] = vec_mine[0] + vec_in[0]
+    vec_steps[1].start()
+    for copy in qkv_copies:
+        copy.wait_recv()
+    for b in range(2):
+        one = jnp.dot(tok_t[...], dqkv[2 * b + core], preferred_element_type=F32)
+        two = jnp.dot(ctx_t[...], dbr[2 * b + core], preferred_element_type=F32)
+        part = jnp.concatenate([one[:, 0:512], one[:, 512:640] + two[:, 0:128], two[:, 128:256]], axis=1).astype(BF16)
+        sums_2[b] = part.reshape(4, 2, 96, 768)
+    for k in (1, 2, 3, 0):
+        first(QKV, k).start()
+    vec_steps[1].wait_recv()
+    vec_mine[2] = vec_mine[1] + vec_in[1]
+    vec_steps[2].start()
+
+    vec_z = [
+        remote(vec_mine.at[3], vec_in.at[3 + z], vec_send.at[2 + k], vec_recv.at[2 + k], at_z[k - 1])
+        for k in (1, 2, 3)
+    ]
+    lag = 2
+    for step in range(len(CHUNKS) + lag):
+        if step < len(CHUNKS):
+            m, k = CHUNKS[step]
+            first(m, k).wait_recv()
+            add_first(m, k)
+            second(m, k).start()
+        if step >= lag:
+            m, k = CHUNKS[step - lag]
+            second(m, k).wait_recv()
+            add_second(m, k)
+            if k:
+                third(m, k).start()
+        if step == 2:
+            vec_steps[2].wait_recv()
+            vec_mine[3] = vec_mine[2] + vec_in[2]
+            for copy in vec_z:
+                copy.start()
+    for copy in vec_z:
+        copy.wait_recv()
+    vec_in[3 + z] = vec_mine[3]
+    vec_out[...] = (vec_in[3] + vec_in[4]) + (vec_in[5] + vec_in[6])
+    for m, out in ((DOWN, down_out), (UP, up_out), (QKV, qkv_out)):
+        for k in (1, 2, 3):
+            third(m, k).wait_recv()
+        total = sums[m][x, z, y].astype(F32)
+        for k in range(3):
+            total = total + in3[m][k].astype(F32)
+        out[...] = total
+    for copy in core_copies + vec_steps + vec_z:
+        copy.wait_send()
+    for m, k in CHUNKS:
+        first(m, k).wait_send()
+        second(m, k).wait_send()
+        if k:
+            third(m, k).wait_send()
+
+
+def reduce_grads(hidden_low, d_pre, active, d_ffn, tokens, d_qkv, context, d_branch, vectors):
+    V = pl.BlockSpec(memory_space=pltpu.VMEM)
+    blocks = {DOWN: (192, 384), UP: (96, 768), QKV: (96, 768)}
+    dma = pltpu.SemaphoreType.DMA
+    return pl.pallas_call(
+        grad_kernel,
+        name="grads",
+        out_shape=(
+            jax.ShapeDtypeStruct((192, 384), F32),
+            jax.ShapeDtypeStruct((96, 768), F32),
+            jax.ShapeDtypeStruct((96, 768), F32),
+            jax.ShapeDtypeStruct((16, 768), F32),
+        ),
+        in_specs=[V] * 9,
+        out_specs=(V,) * 4,
+        scratch_shapes=[
+            pltpu.VMEM((4, 512, 768), BF16),
+            pltpu.VMEM((4, 512, 768), BF16),
+            pltpu.VMEM((4, 192, 512), BF16),
+            pltpu.VMEM((768, 512), BF16),
+            pltpu.VMEM((768, 512), BF16),
+            pltpu.VMEM((768, 512), BF16),
+            pltpu.VMEM((4, 512, 640), BF16),
+            pltpu.VMEM((4, 512, 256), BF16),
+        ]
+        + [pltpu.VMEM((2, 4, 2) + blocks[m], BF16) for m in range(3)]
+        + [pltpu.VMEM((4, 2) + blocks[m], BF16) for m in range(3)]
+        + [pltpu.VMEM((4,) + blocks[m], BF16) for m in range(3)]
+        + [pltpu.VMEM((3,) + blocks[m], BF16) for m in range(3)]
+        + [pltpu.VMEM((4, 16, 768), F32), pltpu.VMEM((7, 16, 768), F32)]
+        + [dma((16,)), dma((16,))]
+        + [dma((3, 4))] * 6
+        + [dma((6,)), dma((6,))],
+        compiler_params=pltpu.CompilerParams(
+            collective_id=1, has_side_effects=True, vmem_limit_bytes=60 * 1024 * 1024
+        ),
+    )(hidden_low, d_pre, active, d_ffn, tokens, d_qkv, context, d_branch, vectors)
+
+
+def local_any(
+    tokens,
+    lengths,
+    cotangent,
+    w_qkv,
+    b_query,
+    b_value,
+    w_out,
+    b_out,
+    first_gain,
+    first_shift,
+    w_up,
+    b_up,
+    w_down,
+    b_down,
+    second_gain,
+    second_shift,
+):
+    lane_count = lax.axis_size("seq")
+    seq_count, part_len, model_width = tokens.shape
+    full_len = part_len * lane_count
+    lane_width = model_width // lane_count
+    head_size = HEAD_DIM
+    heads_here = lane_width // head_size
+    row_count = seq_count * part_len
+    offset = lax.axis_index("seq") * part_len
+    places = offset + jnp.arange(part_len, dtype=jnp.int32)
+    length_row = lengths[0]
+    row_live = (places[None, :] < length_row[:, None]).astype(jnp.float32).reshape(row_count, 1)
+    key_valid = jnp.arange(full_len, dtype=jnp.int32)[None, :] < length_row[:, None]
+    joined_bias = jnp.concatenate([b_query, jnp.zeros_like(b_query), b_value])
+    tokens_flat = tokens.reshape(row_count, model_width)
+    mixed = jnp.dot(tokens_flat, w_qkv, preferred_element_type=jnp.float32) + joined_bias
+    qkv_heads = lax.all_to_all(
+        mixed.astype(jnp.bfloat16).reshape(seq_count, part_len, 3, lane_count, lane_width),
+        "seq",
+        split_axis=3,
+        concat_axis=1,
+        tiled=True,
+    )
+    qkv_heads = qkv_heads.reshape(seq_count, full_len, 3, heads_here, head_size)
+    context_heads, log_total = lax.map(
+        attention_forward_pass,
+        (qkv_heads[:, :, 0], qkv_heads[:, :, 1], qkv_heads[:, :, 2], key_valid),
+    )
+    context_heads = context_heads.reshape(seq_count, full_len, 1, lane_width)
+    context_token_rows = lax.all_to_all(
+        context_heads, "seq", split_axis=1, concat_axis=2, tiled=True
+    ).reshape(row_count, model_width)
+    branch = jnp.dot(context_token_rows, w_out, preferred_element_type=jnp.float32) + b_out
+    normed_one, inverse_one = normalize(tokens_flat.astype(jnp.float32) + branch)
+    hidden = normed_one * first_gain + first_shift
+    hidden_low = hidden.astype(jnp.bfloat16)
+    preactivation_input = jnp.dot(hidden_low, w_up, preferred_element_type=jnp.float32) + b_up
+    active = jax.nn.gelu(preactivation_input, approximate=False).astype(jnp.bfloat16)
+    ffn_out = jnp.dot(active, w_down, preferred_element_type=jnp.float32) + b_down
+    normed_two, inverse_two = normalize(hidden + ffn_out)
+    output_rows = (normed_two * second_gain + second_shift) * row_live
+    output_tokens = output_rows.astype(jnp.bfloat16).reshape(seq_count, part_len, model_width)
+    grad_out = cotangent.reshape(row_count, model_width).astype(jnp.float32) * row_live
+    grad_second_gain = jnp.sum(grad_out * normed_two, axis=0)
+    grad_second_shift = jnp.sum(grad_out, axis=0)
+    d_sum_two = norm_backward(grad_out, normed_two, inverse_two, second_gain)
+    d_ffn = d_sum_two.astype(jnp.bfloat16)
+    grad_b_down = jnp.sum(d_ffn.astype(jnp.float32), axis=0)
+    grad_w_down = contract_rows(active, d_ffn)
+    d_active = times_transposed(d_ffn, w_down)
+    gelu_slope = (
+        0.5 * (1.0 + lax.erf(preactivation_input * ROOT_HALF))
+        + preactivation_input
+        * jnp.exp(-0.5 * preactivation_input * preactivation_input)
+        * INV_ROOT_TWO_PI
+    )
+    d_pre = (d_active * gelu_slope).astype(jnp.bfloat16)
+    grad_b_up = jnp.sum(d_pre.astype(jnp.float32), axis=0)
+    grad_w_up = contract_rows(hidden_low, d_pre)
+    d_hidden = d_sum_two + times_transposed(d_pre, w_up)
+    grad_first_gain = jnp.sum(d_hidden * normed_one, axis=0)
+    grad_first_shift = jnp.sum(d_hidden, axis=0)
+    d_sum_one = norm_backward(d_hidden, normed_one, inverse_one, first_gain)
+    d_branch = d_sum_one.astype(jnp.bfloat16)
+    grad_b_out = jnp.sum(d_branch.astype(jnp.float32), axis=0)
+    grad_w_out = contract_rows(context_token_rows, d_branch)
+    d_context = times_transposed(d_branch, w_out).astype(jnp.bfloat16)
+    d_context = d_context.reshape(seq_count, part_len, lane_count, lane_width)
+    d_context_heads = lax.all_to_all(d_context, "seq", split_axis=2, concat_axis=1, tiled=True)
+    d_context_heads = d_context_heads.reshape(seq_count, full_len, heads_here, head_size)
+    d_qkv_heads = lax.map(
+        attend_backward,
+        (
+            qkv_heads[:, :, 0],
+            qkv_heads[:, :, 1],
+            qkv_heads[:, :, 2],
+            key_valid,
+            log_total,
+            d_context_heads,
+        ),
+    )
+    d_qkv_heads = d_qkv_heads.reshape(seq_count, full_len, 3, 1, lane_width)
+    d_qkv = lax.all_to_all(d_qkv_heads, "seq", split_axis=1, concat_axis=3, tiled=True).reshape(
+        row_count, 3 * model_width
+    )
+    d_qkv_wide = d_qkv.astype(jnp.float32)
+    grad_b_query = jnp.sum(d_qkv_wide[:, :model_width], axis=0)
+    grad_b_value = jnp.sum(d_qkv_wide[:, 2 * model_width :], axis=0)
+    grad_w_qkv = contract_rows(tokens_flat, d_qkv)
+    grad_rows = d_sum_one + times_transposed(d_qkv, w_qkv)
+    grad_tokens = grad_rows.astype(jnp.bfloat16).reshape(seq_count, part_len, model_width)
+    matrices = (grad_w_qkv, grad_w_out, grad_w_up, grad_w_down)
+    halfway = (
+        lax.psum_scatter(matrices[0], "dp", scatter_dimension=0, tiled=True),
+        lax.psum_scatter(matrices[1], "dp", scatter_dimension=0, tiled=True),
+        lax.psum_scatter(matrices[2], "dp", scatter_dimension=0, tiled=True),
+        lax.psum_scatter(matrices[3], "dp", scatter_dimension=0, tiled=True),
+    )
+    matrices = (
+        lax.psum_scatter(
+            halfway[0].astype(jnp.bfloat16), "seq", scatter_dimension=1, tiled=True
+        ).astype(jnp.float32),
+        lax.psum_scatter(
+            halfway[1].astype(jnp.bfloat16), "seq", scatter_dimension=1, tiled=True
+        ).astype(jnp.float32),
+        lax.psum_scatter(
+            halfway[2].astype(jnp.bfloat16), "seq", scatter_dimension=1, tiled=True
+        ).astype(jnp.float32),
+        lax.psum_scatter(
+            halfway[3].astype(jnp.bfloat16), "seq", scatter_dimension=1, tiled=True
+        ).astype(jnp.float32),
+    )
+    vectors = lax.psum(
+        (
+            grad_b_query,
+            grad_b_value,
+            grad_b_out,
+            grad_first_gain,
+            grad_first_shift,
+            grad_b_up,
+            grad_b_down,
+            grad_second_gain,
+            grad_second_shift,
+        ),
+        ("dp", "seq"),
+    )
+    return (
+        output_tokens,
+        grad_tokens,
+        matrices[0],
+        matrices[1],
+        matrices[2],
+        matrices[3],
+        vectors[0],
+        vectors[1],
+        vectors[2],
+        vectors[3],
+        vectors[4],
+        vectors[5],
+        vectors[6],
+        vectors[7],
+        vectors[8],
+    )
 
 
 def local(
@@ -150,7 +556,6 @@
     d_sum_two = norm_backward(grad_out, normed_two, inverse_two, second_gain)
     d_ffn = d_sum_two.astype(jnp.bfloat16)
     grad_b_down = jnp.sum(d_ffn.astype(jnp.float32), axis=0)
-    grad_w_down = contract_rows(active, d_ffn)
     d_active = times_transposed(d_ffn, w_down)
     gelu_slope = (
         0.5 * (1.0 + lax.erf(preactivation_input * ROOT_HALF))
@@ -160,14 +565,12 @@
     )
     d_pre = (d_active * gelu_slope).astype(jnp.bfloat16)
     grad_b_up = jnp.sum(d_pre.astype(jnp.float32), axis=0)
-    grad_w_up = contract_rows(hidden_low, d_pre)
     d_hidden = d_sum_two + times_transposed(d_pre, w_up)
     grad_first_gain = jnp.sum(d_hidden * normed_one, axis=0)
     grad_first_shift = jnp.sum(d_hidden, axis=0)
     d_sum_one = norm_backward(d_hidden, normed_one, inverse_one, first_gain)
     d_branch = d_sum_one.astype(jnp.bfloat16)
     grad_b_out = jnp.sum(d_branch.astype(jnp.float32), axis=0)
-    grad_w_out = contract_rows(context_token_rows, d_branch)
     d_context = times_transposed(d_branch, w_out).astype(jnp.bfloat16)
     d_context = d_context.reshape(seq_count, part_len, lane_count, lane_width)
     d_context_heads = lax.all_to_all(d_context, "seq", split_axis=2, concat_axis=1, tiled=True)
@@ -190,60 +593,41 @@
     d_qkv_wide = d_qkv.astype(jnp.float32)
     grad_b_query = jnp.sum(d_qkv_wide[:, :model_width], axis=0)
     grad_b_value = jnp.sum(d_qkv_wide[:, 2 * model_width :], axis=0)
-    grad_w_qkv = contract_rows(tokens_flat, d_qkv)
     grad_rows = d_sum_one + times_transposed(d_qkv, w_qkv)
     grad_tokens = grad_rows.astype(jnp.bfloat16).reshape(seq_count, part_len, model_width)
-    matrices = (grad_w_qkv, grad_w_out, grad_w_up, grad_w_down)
-    halfway = (
-        lax.psum_scatter(matrices[0], "dp", scatter_dimension=0, tiled=True),
-        lax.psum_scatter(matrices[1], "dp", scatter_dimension=0, tiled=True),
-        lax.psum_scatter(matrices[2], "dp", scatter_dimension=0, tiled=True),
-        lax.psum_scatter(matrices[3], "dp", scatter_dimension=0, tiled=True),
-    )
-    matrices = (
-        lax.psum_scatter(
-            halfway[0].astype(jnp.bfloat16), "seq", scatter_dimension=1, tiled=True
-        ).astype(jnp.float32),
-        lax.psum_scatter(
-            halfway[1].astype(jnp.bfloat16), "seq", scatter_dimension=1, tiled=True
-        ).astype(jnp.float32),
-        lax.psum_scatter(
-            halfway[2].astype(jnp.bfloat16), "seq", scatter_dimension=1, tiled=True
-        ).astype(jnp.float32),
-        lax.psum_scatter(
-            halfway[3].astype(jnp.bfloat16), "seq", scatter_dimension=1, tiled=True
-        ).astype(jnp.float32),
-    )
-    vectors = lax.psum(
-        (
+    vectors = jnp.concatenate(
+        [
             grad_b_query,
             grad_b_value,
             grad_b_out,
             grad_first_gain,
             grad_first_shift,
-            grad_b_up,
             grad_b_down,
             grad_second_gain,
             grad_second_shift,
-        ),
-        ("dp", "seq"),
+            grad_b_up,
+            jnp.zeros((4 * model_width,), jnp.float32),
+        ]
+    ).reshape(16, model_width)
+    down, up, joined, vectors = reduce_grads(
+        hidden_low, d_pre, active, d_ffn, tokens_flat, d_qkv, context_token_rows, d_branch, vectors
     )
     return (
         output_tokens,
         grad_tokens,
-        matrices[0],
-        matrices[1],
-        matrices[2],
-        matrices[3],
+        joined[:, :576],
+        joined[:, 576:],
+        up,
+        down.T,
         vectors[0],
         vectors[1],
         vectors[2],
         vectors[3],
         vectors[4],
+        vectors[8:12].reshape(-1),
         vectors[5],
         vectors[6],
         vectors[7],
-        vectors[8],
     )
 
 
@@ -283,4 +667,5 @@
         P(),
         P(),
     )
-    return jax.shard_map(local, mesh=mesh, in_specs=in_specs, out_specs=out_specs, check_vma=False)
+    return jax.shard_map(
+        local if dict(mesh.shape) == {"dp": 8, "seq": 4} else local_any, mesh=mesh, in_specs=in_specs, out_specs=out_specs, check_vma=False)

time: 760 us -> 300 us (0.39)
  waiting for transfers between devices: 504 us -> 46.3 us
  Pallas kernels: 0 us -> 99.9 us
  blocking collectives: 65.6 us -> 0 us
  matrix products: 63.9 us -> 41.7 us
  between operations: 14.6 us -> 1.1 us
  other arithmetic: 25.5 us -> 15.6 us
    reduce_scatter x5 -> x0, waiting for transfers between devices: 347 us -> none  [the longest x1 164 us: local(): lax.psum_scatter(matrices[3], 'dp', scatter_dimension=0, tiled=True)]
    unnamed x11 -> x0, waiting for transfers between devices: 132 us -> none
    pallas_call x0 -> x1, Pallas kernels: none -> 99.9 us  [reduce_grads(): pl.pallas_call(grad_kernel, name='grads', out_shape=(jax.ShapeDtypeStruct...]
    psum x1 -> x0, blocking collectives: 41.1 us -> none  [local(): lax.psum((grad_b_query, grad_b_value, grad_b_out, grad_first_gain, grad_f...]
    all_to_all x1 -> x0, blocking collectives: 24.5 us -> none  [local(): lax.all_to_all(d_qkv_heads, 'seq', split_axis=1, concat_axis=3, tiled=True)]
    dot_general x4 -> x0, matrix products: 21.7 us -> none  [contract_rows(): lax.dot_general(left, right, (((0,), (0,)), ((), ())), preferred_element_...]
    all_to_all x0 -> x1, waiting for transfers between devices: none -> 16.2 us  [local(): lax.all_to_all(d_qkv_heads, 'seq', split_axis=1, concat_axis=3, tiled=True)]
    convert_element_type x5 -> x1, other arithmetic: 9.05 us -> 0.2 us  [local(): hidden_low = hidden.astype(jnp.bfloat16)]
  transfers between devices with their start and end apart: 11 -> 4, of which waited for: 8 -> 4; matrix products, arithmetic and copies ran while one was open for 12% -> 2% of each run, Pallas kernels for 0% -> 0%
where the time goes in v1:
time: 300 us; the launch traced here: 297 us
  Pallas kernels  99.9 us (33%)
  local copies, waits for them, and re-layouts  74.8 us (25%)
  waiting for transfers between devices  46.3 us (15%)
  matrix products  41.7 us (14%)
  starting transfers between devices  17.3 us (6%)
  other arithmetic  15.6 us (5%)
    pallas_call x1, Pallas kernels, reduce_grads(): pl.pallas_call(grad_kernel, name='grads', out_shape=(jax.ShapeDtypeStruct...  99.9 us
    unnamed x70, local copies, waits for them, and re-layouts  16.3 us
    all_to_all x1, waiting for transfers between devices, local(): lax.all_to_all(d_qkv_heads, 'seq', split_axis=1, concat_axis=3, tiled=True)  16.2 us
    all_to_all x1, waiting for transfers between devices, local(): lax.all_to_all(mixed.astype(jnp.bfloat16).reshape(seq_count, part_len, 3,...  15.8 us
    dot_general x4, matrix products, times_transposed(): lax.dot_general(left, weight_matrix, (((1,), (1,)), ((), ())), preferred_...  9.87 us
    reshape x2, local copies, waits for them, and re-layouts, local(): mixed.astype(jnp.bfloat16)  9.58 us
    dot_general x1, matrix products, local(): jnp.dot(hidden_low, w_up, preferred_element_type=jnp.float32) + b_up  9.25 us
    all_to_all x2, local copies, waits for them, and re-layouts, local(): lax.all_to_all(d_qkv_heads, 'seq', split_axis=1, concat_axis=3, tiled=True)  7.57 us
  transfers between devices with their start and end apart: 4, of which 4 were waited for; matrix products, arithmetic and copies ran while one was open for 2% of the time, Pallas kernels for 0%

profile of v1, /device:TPU:0, one launch (start us, length us, event | category | flops | bytes accessed | tf_op | source)
XLA Modules:
  0.0 296.7 jit_solution(12972981945609630097)
XLA Ops:
  2.7 3.1 %fusion.50 = bf16[256,2304]{1,0:T(8,128)(2,1)} fusion(bf16[256,768]{1,0:T(8,128)(2,1)} %bitcast.179, bf16[768,2304]{1,0:T(8,128)(2,1)S(1)} %copy-done, f32[2304]{0:T(1024)S(1)} %pad_maximum_fusion), kind=kOutput, calls=%fused_computation.64 | convolution fusion | flops 907149312 | bytes 5121024 | tf_op jit(solution)/shard_map/dot_general | solution.py:526
  5.8 4.4 %reshape.260 = bf16[2,128,3,4,192]{4,3,2,1,0:T(4,128)(2,1)} reshape(bf16[256,2304]{1,0:T(8,128)(2,1)} %fusion.50) | data formatting | bytes 2359296 | tf_op jit(solution)/shard_map/reshape | solution.py:528
  10.2 5.2 %copy.98 = bf16[2,128,3,4,192]{1,0,4,2,3:T(2,128)(2,1)} copy(bf16[2,128,3,4,192]{4,3,2,1,0:T(4,128)(2,1)} %reshape.260) | data formatting | bytes 2359296 | tf_op jit(solution)/shard_map/reshape | solution.py:528
  15.4 4.3 %all-to-all-start = ((bf16[2,128,3,4,192]{1,0,4,2,3:T(2,128)(2,1)}), bf16[2,128,3,4,192]{1,0,4,2,3:T(2,128)(2,1)}, u32[]{:S(2)}, u32[]{:S(2)}) async-start(bf16[2,128,3,4,192]{1,0,4,2,3:T(2,128)(2,1)} %copy.98), calls=%async_computation | async-start | bytes 2359296 | tf_op jit(solution)/shard_map/all_to_all | solution.py:527
  20.4 15.8 %all-to-all-done = bf16[2,128,3,4,192]{1,0,4,2,3:T(2,128)(2,1)} async-done(((bf16[2,128,3,4,192]{1,0,4,2,3:T(2,128)(2,1)}), bf16[2,128,3,4,192]{1,0,4,2,3:T(2,128)(2,1)}, u32[]{:S(2)}, u32[]{:S(2)}) %all-to-all-start) | async-done | bytes 1179680 | tf_op jit(solution)/shard_map/all_to_all | solution.py:527
  36.2 3.2 %copy.99 = bf16[2,4,128,3,1,192]{2,1,5,3,0,4:T(4,128)(2,1)} copy(bf16[2,4,128,3,1,192]{2,0,5,3,1,4:T(2,128)(2,1)} %bitcast.19) | data formatting | bytes 2359296 | tf_op jit(solution)/shard_map/all_to_all | solution.py:527
  39.4 3.2 %reshape.247 = bf16[2,512,3,3,64]{1,4,3,2,0:T(8,128)(2,1)} reshape(bf16[2,4,128,3,1,192]{2,1,5,3,0,4:T(4,128)(2,1)} %copy.99) | data formatting | bytes 2359296 | tf_op jit(solution)/shard_map/reshape | solution.py:534
  42.6 2.3 slice_bitcast_fusion
  44.9 9.6 %while.22 = (s32[]{:T(128)}, bf16[2,512,3,64]{1,3,2,0:T(8,128)(2,1)}, f32[2,3,512]{2,1,0:T(4,128)}, bf16[2,512,3,64]{1,3,2,0:T(8,128)(2,1)}, pred[2,512]{1,0:T(4...) while((s32[]{:T(128)}, ...), condition=%wide.region_3.4_spmd, body=%wide.region_0.3_spmd.sunk | while | flops 210860544 | bytes 11857013 | solution.py:535
  54.6 2.0 copy.100
  56.6 4.3 %all-to-all-start.1 = ((bf16[2,512,1,192]{3,0,2,1:T(2,128)(2,1)}), bf16[2,512,1,192]{3,0,2,1:T(2,128)(2,1)}, u32[]{:S(2)}, u32[]{:S(2)}) async-start(bf16[2,512,1,192]{3,0,2,1:T(2,128)(2,1)} %copy.100), calls=%async_computation.1 | async-start | bytes 1048576 | tf_op jit(solution)/shard_map/all_to_all | solution.py:540
  62.8 6.9 %all-to-all-done.1 = bf16[2,512,1,192]{3,0,2,1:T(2,128)(2,1)} async-done(((bf16[2,512,1,192]{3,0,2,1:T(2,128)(2,1)}), bf16[2,512,1,192]{3,0,2,1:T(2,128)(2,1)}, u32[]{:S(2)}, u32[]{:S(2)}) %all-to-all-start.1) | async-done | bytes 393248 | tf_op jit(solution)/shard_map/all_to_all | solution.py:540
  69.6 2.1 copy.116
  73.3 2.1 fusion.73
  76.0 9.2 %fusion.53 = (bf16[256,3072]{1,0:T(8,128)(2,1)S(1)}, f32[256,3072]{1,0:T(8,128)S(1)}) fusion(f32[3072]{0:T(1024)S(1)} %copy-done.29, bf16[256,768]{1,0:T(8,128)(2,1)S(1)} %fusion.70.hid_ref, bf16[768,3072]{1,0:T(8,128)(2,1)S(1)} %copy-done.28), kind=kOutput, calls=%fused_computation.67 | convolution fusion | flops 1259864064 | bytes 9842688 | tf_op jit(solution)/shard_map/dot_general | solution.py:547
  89.9 3.0 %convert_reduce_fusion = (f32[3072]{0:T(1024)}, bf16[256,3072]{1,0:T(8,128)(2,1)S(1)}) fusion(f32[256,3072]{1,0:T(8,128)S(1)} %get-tuple-element.175, bf16[256,768]{1,0:T(8,128)(2,1)S(1)} %get-tuple-element.155.dffn_ref, bf16[3072,768]{1,0:T(8,128)(2,1)S(1)} %bitcast.187), kind=kOutput, calls=%fused_computation.72 | convolution fusion | flops 1217393664 | bytes 9842688 | tf_op jit(solution)/shard_map/dot_general | solution.py:29
  92.9 2.2 multiply_reduce_fusion.2
  98.3 1.9 copy.103
  102.1 4.1 %all-to-all-start.2 = ((bf16[2,128,4,192]{1,0,3,2:T(2,128)(2,1)}), bf16[2,128,4,192]{1,0,3,2:T(2,128)(2,1)}, u32[]{:S(2)}, u32[]{:S(2)}) async-start(bf16[2,128,4,192]{1,0,3,2:T(2,128)(2,1)} %reshape.251), calls=%async_computation.2 | async-start | bytes 786432 | tf_op jit(solution)/shard_map/all_to_all | solution.py:576
  106.2 7.5 %all-to-all-done.2 = bf16[2,128,4,192]{1,0,3,2:T(2,128)(2,1)} async-done(((bf16[2,128,4,192]{1,0,3,2:T(2,128)(2,1)}), bf16[2,128,4,192]{1,0,3,2:T(2,128)(2,1)}, u32[]{:S(2)}, u32[]{:S(2)}) %all-to-all-start.2) | async-done | bytes 393248 | tf_op jit(solution)/shard_map/all_to_all | solution.py:576
  113.7 2.0 copy.104
  115.8 1.9 reshape.252
  117.7 13.8 %while.23 = (s32[]{:T(128)}, bf16[2,512,3,3,64]{1,4,3,2,0:T(8,128)(2,1)}, bf16[2,512,3,64]{1,3,2,0:T(8,128)(2,1)}, pred[2,512]{1,0:T(4,128)(4,1)S(1)}, bf16[2,51...) while((s32[]{:T(128)}, ...), condition=%wide.region_14.15_spmd, body=%wide.region_12.14_spmd.sunk | while | flops 512653824 | bytes 31494340 | solution.py:578
  131.5 4.9 %copy.105 = bf16[2,512,3,1,192]{4,0,3,2,1:T(2,128)(2,1)} copy(bf16[2,512,3,1,192]{1,4,3,2,0:T(8,128)(2,1)} %bitcast.33) | data formatting | bytes 2359296 | tf_op jit(solution)/shard_map/reshape | solution.py:589
  136.4 4.6 %all-to-all-start.3 = ((bf16[2,512,3,1,192]{4,0,3,2,1:T(2,128)(2,1)}), bf16[2,512,3,1,192]{4,0,3,2,1:T(2,128)(2,1)}, u32[]{:S(2)}, u32[]{:S(2)}) async-start(bf16[2,512,3,1,192]{4,0,3,2,1:T(2,128)(2,1)} %copy.105), calls=%async_computation.3 | async-start | bytes 3145728 | tf_op jit(solution)/shard_map/all_to_all | solution.py:590
  142.8 1.9 copy.109.ctx_ref
  144.7 16.2 %all-to-all-done.3 = bf16[2,512,3,1,192]{4,0,3,2,1:T(2,128)(2,1)} async-done(((bf16[2,512,3,1,192]{4,0,3,2,1:T(2,128)(2,1)}), bf16[2,512,3,1,192]{4,0,3,2,1:T(2,128)(2,1)}, u32[]{:S(2)}, u32[]{:S(2)}) %all-to-all-start.3) | async-done | bytes 1179680 | tf_op jit(solution)/shard_map/all_to_all | solution.py:590
  160.9 5.1 %copy.117 = bf16[2,4,128,3,1,192]{2,1,5,3,0,4:T(4,128)(2,1)} copy(bf16[2,4,128,3,1,192]{5,0,3,2,1,4:T(2,128)(2,1)} %bitcast.34) | data formatting | bytes 2359296 | tf_op jit(solution)/shard_map/all_to_all | solution.py:590
  166.0 2.5 copy.107
  183.3 2.4 copy.108.dqkv_ref
  185.6 99.9 %grads.1 = (f32[192,384]{1,0:T(8,128)}, f32[96,768]{1,0:T(8,128)}, f32[96,768]{1,0:T(8,128)}, f32[16,768]{1,0:T(8,128)}) custom-call(bf16[256,768]{1,0:T(8,128)(2,1)} %copy-done.9, bf16[256,3072]{1,0:T(8,128)(2,1)} %copy-done.12, bf16[256,3072]{1,0:T(8,128)(2,1)} %copy-done.11, bf16[256,768]{1,0:T(8,128)(2,1)} %copy-done.8, bf16[256,768]{1,0:T(8,128)(2,1)} %bitcast.181, ...), custom_call_target="tpu_custom_call" | custom-call | tf_op jit(solution)/shard_map/grads/pallas_call | solution.py:297
  291.8 3.4 %fusion.67 = bf16[256,768]{1,0:T(8,128)(2,1)} fusion(f32[256,768]{1,0:T(8,128)} %get-tuple-element.159, bf16[768,2304]{1,0:T(8,128)(2,1)S(1)} %copy-done, bf16[288,8,2,128]{3,2,1,0:T(2,128)(2,1)} %bitcast.173), kind=kOutput, calls=%fused_computation.94 | convolution fusion | flops 906362880 | bytes 5898240 | tf_op jit(solution)/shard_map/dot_general | solution.py:29
  (151 shorter events, 63.8 us)
Async XLA Ops:
  10.2 9.5 %copy-start.27 = (s32[1,2]{1,0:T(1,128)S(1)}, s32[1,2]{1,0:T(1,128)}, u32[]{:S(2)}) copy-start(s32[1,2]{1,0:T(1,128)} %param.21) | copy-start | bytes 28
  15.4 20.8 %all-to-all-start = ((bf16[2,128,3,4,192]{1,0,4,2,3:T(2,128)(2,1)}), bf16[2,128,3,4,192]{1,0,4,2,3:T(2,128)(2,1)}, u32[]{:S(2)}, u32[]{:S(2)}) async-start(bf16[2,128,3,4,192]{1,0,4,2,3:T(2,128)(2,1)} %copy.98), calls=%async_computation | async-start | bytes 2359296 | tf_op jit(solution)/shard_map/all_to_all | solution.py:527
  44.9 16.0 %copy-start.16 = (f32[768]{0:T(1024)S(1)}, f32[768]{0:T(1024)}, u32[]{:S(2)}) copy-start(f32[768]{0:T(1024)} %param.34) | copy-start | bytes 9220
  45.0 3.2 %copy-start.4 = (bf16[2,512,3,64]{1,3,2,0:T(8,128)(2,1)S(1)}, bf16[2,512,3,64]{1,3,2,0:T(8,128)(2,1)}, u32[]{:S(2)}) copy-start(bf16[2,512,3,64]{1,3,2,0:T(8,128)(2,1)} %get-tuple-element.302) | copy-start | bytes 1179652 | tf_op jit(solution)/shard_map/while
  49.8 3.2 %copy-start.4 = (bf16[2,512,3,64]{1,3,2,0:T(8,128)(2,1)S(1)}, bf16[2,512,3,64]{1,3,2,0:T(8,128)(2,1)}, u32[]{:S(2)}) copy-start(bf16[2,512,3,64]{1,3,2,0:T(8,128)(2,1)} %get-tuple-element.302) | copy-start | bytes 1179652 | tf_op jit(solution)/shard_map/while
  56.6 13.0 %all-to-all-start.1 = ((bf16[2,512,1,192]{3,0,2,1:T(2,128)(2,1)}), bf16[2,512,1,192]{3,0,2,1:T(2,128)(2,1)}, u32[]{:S(2)}, u32[]{:S(2)}) async-start(bf16[2,512,1,192]{3,0,2,1:T(2,128)(2,1)} %copy.100), calls=%async_computation.1 | async-start | bytes 1048576 | tf_op jit(solution)/shard_map/all_to_all | solution.py:540
  60.9 14.8 %copy-start.17 = (f32[768]{0:T(1024)S(1)}, f32[768]{0:T(1024)}, u32[]{:S(2)}) copy-start(f32[768]{0:T(1024)} %param.28) | copy-start | bytes 9220
  71.7 4.0 %copy-start.23 = (f32[768]{0:T(1024)S(1)}, f32[768]{0:T(1024)}, u32[]{:S(2)}) copy-start(f32[768]{0:T(1024)} %param.29) | copy-start | bytes 9220
  71.7 4.2 %copy-start.28 = (bf16[768,3072]{1,0:T(8,128)(2,1)S(1)}, bf16[768,3072]{1,0:T(8,128)(2,1)}, u32[]{:S(2)}) copy-start(bf16[768,3072]{1,0:T(8,128)(2,1)} %param.30) | copy-start | bytes 14155780
  71.7 4.2 %copy-start.29 = (f32[3072]{0:T(1024)S(1)}, f32[3072]{0:T(1024)}, u32[]{:S(2)}) copy-start(f32[3072]{0:T(1024)} %param.31) | copy-start | bytes 36868
  73.3 2.4 copy-start.10
  73.3 12.0 %slice-start = ((s8[4718592]{0:T(1024)(128)(4,1)}), s8[4194304]{0:T(1024)(128)(4,1)S(1)}, s32[]{:S(2)}) async-start(s8[4718592]{0:T(1024)(128)(4,1)} %bitcast.186), calls=%async_computation.4 | async-start | bytes 8388608
  76.0 9.3 %copy-start.9 = (bf16[256,768]{1,0:T(8,128)(2,1)}, bf16[256,768]{1,0:T(8,128)(2,1)S(1)}, u32[]{:S(2)}) copy-start(bf16[256,768]{1,0:T(8,128)(2,1)S(1)} %fusion.70.hid_ref) | copy-start | bytes 1179652
  76.0 9.3 %slice-start.1 = ((s8[4718592]{0:T(1024)(128)(4,1)}), s8[524288]{0:T(1024)(128)(4,1)S(1)}, s32[]{:S(2)}) async-start(s8[4718592]{0:T(1024)(128)(4,1)} %bitcast.186), calls=%async_computation.5 | async-start | bytes 1048576
  76.0 9.3 %copy-start.30 = (f32[768]{0:T(1024)S(1)}, f32[768]{0:T(1024)}, u32[]{:S(2)}) copy-start(f32[768]{0:T(1024)} %param.33) | copy-start | bytes 9220
  85.3 2.8 copy-start.22
  85.3 2.8 copy-start.24
  89.9 3.0 %copy-start.8 = (bf16[256,768]{1,0:T(8,128)(2,1)}, bf16[256,768]{1,0:T(8,128)(2,1)S(1)}, u32[]{:S(2)}) copy-start(bf16[256,768]{1,0:T(8,128)(2,1)S(1)} %get-tuple-element.155.dffn_ref) | copy-start | bytes 1179652
  92.9 4.2 %copy-start.13 = (bf16[768,768]{1,0:T(8,128)(2,1)S(1)}, bf16[768,768]{1,0:T(8,128)(2,1)}, u32[]{:S(2)}) copy-start(bf16[768,768]{1,0:T(8,128)(2,1)} %param.26) | copy-start | bytes 3538948
  102.1 11.6 %all-to-all-start.2 = ((bf16[2,128,4,192]{1,0,3,2:T(2,128)(2,1)}), bf16[2,128,4,192]{1,0,3,2:T(2,128)(2,1)}, u32[]{:S(2)}, u32[]{:S(2)}) async-start(bf16[2,128,4,192]{1,0,3,2:T(2,128)(2,1)} %reshape.251), calls=%async_computation.2 | async-start | bytes 786432 | tf_op jit(solution)/shard_map/all_to_all | solution.py:576
  117.7 2.4 copy-start.1
  117.7 2.4 copy-start.2
  124.6 2.4 copy-start.1
  124.6 2.4 copy-start.2
  136.4 24.5 %all-to-all-start.3 = ((bf16[2,512,3,1,192]{4,0,3,2,1:T(2,128)(2,1)}), bf16[2,512,3,1,192]{4,0,3,2,1:T(2,128)(2,1)}, u32[]{:S(2)}, u32[]{:S(2)}) async-start(bf16[2,512,3,1,192]{4,0,3,2,1:T(2,128)(2,1)} %copy.105), calls=%async_computation.3 | async-start | bytes 3145728 | tf_op jit(solution)/shard_map/all_to_all | solution.py:590
  168.5 5.6 %copy-start.26 = (f32[768]{0:T(1024)S(1)}, f32[768]{0:T(1024)}, u32[]{:S(2)}) copy-start(f32[768]{0:T(1024)} %get-tuple-element.108) | copy-start | bytes 9220
  168.5 6.9 %copy-start.25 = (f32[768]{0:T(1024)S(1)}, f32[768]{0:T(1024)}, u32[]{:S(2)}) copy-start(f32[768]{0:T(1024)} %get-tuple-element.113) | copy-start | bytes 9220
  168.5 8.2 %copy-start.19 = (f32[768]{0:T(1024)S(1)}, f32[768]{0:T(1024)}, u32[]{:S(2)}) copy-start(f32[768]{0:T(1024)} %get-tuple-element.154) | copy-start | bytes 9220
  168.5 9.5 %copy-start.18 = (f32[768]{0:T(1024)S(1)}, f32[768]{0:T(1024)}, u32[]{:S(2)}) copy-start(f32[768]{0:T(1024)} %get-tuple-element.110) | copy-start | bytes 9220
  168.5 12.1 %copy-start.20 = (f32[3072]{0:T(1024)S(1)}, f32[3072]{0:T(1024)}, u32[]{:S(2)}) copy-start(f32[3072]{0:T(1024)} %get-tuple-element.179) | copy-start | bytes 36868
  291.8 3.4 %copy-start.15 = (f32[96,768]{1,0:T(8,128)S(1)}, f32[96,768]{1,0:T(8,128)}, u32[]{:S(2)}) copy-start(f32[96,768]{1,0:T(8,128)} %get-tuple-element.353) | copy-start | bytes 884740
  291.8 4.1 %copy-start.14 = (f32[192,384]{1,0:T(8,128)S(1)}, f32[192,384]{1,0:T(8,128)}, u32[]{:S(2)}) copy-start(f32[192,384]{1,0:T(8,128)} %get-tuple-element.104) | copy-start | bytes 884740
  (9 other events, 14.1 us)

commit v2 on v0

--- a/solution.py
+++ b/solution.py
@@ -1,7 +1,15 @@
+import functools
+
 import jax
 import jax.numpy as jnp
 from jax import lax
+from jax.experimental import pallas as pl
+from jax.experimental.pallas import tpu as pltpu
 from jax.sharding import PartitionSpec as P
+
+MESH_ID = pl.DeviceIdType.MESH
+BF16 = jnp.bfloat16
+F32 = jnp.float32
 
 HEAD_DIM = 64
 
@@ -85,7 +93,7 @@
     return jnp.stack([grad_queries, grad_keys, grad_values], axis=1).astype(jnp.bfloat16)
 
 
-def local(
+def local_any(
     tokens,
     lengths,
     cotangent,
@@ -247,6 +255,542 @@
     )
 
 
+DOWN, UP, QKV = 0, 1, 2
+ORDER = (1, 2, 3, 0)
+CHUNKS = tuple((m, k) for k in ORDER for m in (DOWN, UP)) + tuple((QKV, k) for k in ORDER)
+X_FIRST = {(UP, 0), (UP, 1), (UP, 2), (UP, 3), (QKV, 2), (QKV, 0)}
+BLOCKS = ((192, 384), (96, 768), (96, 768))
+
+B_QUERY, B_VALUE, B_OUT, FIRST_GAIN, FIRST_SHIFT, B_DOWN, SECOND_GAIN, SECOND_SHIFT, B_UP = range(9)
+
+ROWS = 256
+PART = 128
+WIDTH = 768
+STEP = 32
+
+
+def place():
+    row, lane = lax.axis_index("dp"), lax.axis_index("seq")
+    return row // 2, row % 2, lane // 2, lane % 2
+
+
+def device(z, y, x, core):
+    return (z * 2 + y, x * 2 + core)
+
+
+def remote(source, target, send, receive, where):
+    return pltpu.make_async_remote_copy(
+        src_ref=source,
+        dst_ref=target,
+        send_sem=send,
+        recv_sem=receive,
+        device_id=where,
+        device_id_type=MESH_ID,
+    )
+
+
+def dot(left, right):
+    return jnp.dot(left, right, preferred_element_type=F32)
+
+
+def dot_t(left, right):
+    return lax.dot_general(left, right, (((1,), (1,)), ((), ())), preferred_element_type=F32)
+
+
+def fold(rows):
+    return jnp.sum(rows.reshape(rows.shape[0] // 8, 8, rows.shape[1]), axis=0)
+
+
+def mean(rows):
+    return jnp.sum(rows, axis=-1, keepdims=True) * (1.0 / WIDTH)
+
+
+def layer_kernel(
+    tokens_in, lengths_in, cot_in, w_qkv_in, w_out_in, w_up_in, w_down_in,
+    b_query_in, b_value_in, b_out_in, first_gain_in, first_shift_in, b_up_in, b_down_in, second_gain_in, second_shift_in,
+    tokens_out, grad_out, down_out, up_out, qkv_out, vec_out,
+    w_qkv, w_out, w_up, w_down, par, tok, cot, q3, k3, v3, bias, probs, hidden, xhat, rstd, low, slope, wide, total,
+    dsum, dctx3, dkv_own, dkv_send, dkv_in, dq_t, dqkv_flat, out_rows, grad_rows,
+    act, dpre, dffn_t, hid_t, tok_t, ctx_t, dqkv, dbr,
+    sums_0, sums_1, sums_2, in1_0, in1_1, in1_2, in2_0, in2_1, in2_2, in3_0, in3_1, in3_2,
+    vec_mine, vec_in,
+    load, ex_send, ex_recv, core_send, core_recv, act_send, act_recv,
+    send1, recv1, send2, recv2, send3, recv3, vec_send, vec_recv,
+):
+    z, y, x, core = place()
+    sums, in1, in2, in3 = (sums_0, sums_1, sums_2), (in1_0, in1_1, in1_2), (in2_0, in2_1, in2_2), (in3_0, in3_1, in3_2)
+    at_core = device(z, y, x, 1 - core)
+    at_x = device(z, y, 1 - x, core)
+    at_y = device(z, 1 - y, x, core)
+    at_z = [device((z + k) % 4, y, x, core) for k in (1, 2, 3)]
+
+    loads = [pltpu.make_async_copy(tokens_in.at[x], tok.at[pl.ds(0, PART)], load.at[0])]
+    for n, s in enumerate((1, 2, 0)):
+        loads.append(
+            pltpu.make_async_copy(
+                w_qkv_in.at[:, pl.ds(WIDTH * s, WIDTH)], w_qkv.at[:, pl.ds(WIDTH * s, WIDTH)], load.at[1 + n]
+            )
+        )
+    loads.append(pltpu.make_async_copy(cot_in.at[x], cot.at[pl.ds(0, PART)], load.at[4]))
+    loads.append(pltpu.make_async_copy(w_out_in, w_out, load.at[5]))
+    for t in range(4):
+        loads.append(pltpu.make_async_copy(w_up_in.at[:, pl.ds(WIDTH * t, WIDTH)], w_up.at[t], load.at[6 + t]))
+    for t in range(4):
+        loads.append(pltpu.make_async_copy(w_down_in.at[pl.ds(WIDTH * t, WIDTH)], w_down.at[t], load.at[10 + t]))
+    for copy in loads:
+        copy.start()
+
+    barrier = pltpu.get_barrier_semaphore()
+    for where in [at_core, at_x, at_y] + at_z:
+        pl.semaphore_signal(barrier, inc=1, device_id=where, device_id_type=MESH_ID)
+    pl.semaphore_wait(barrier, 6)
+
+    get_tok = remote(tokens_in.at[1 - x], tok.at[pl.ds(PART, PART)], ex_send.at[0], ex_recv.at[0], at_x)
+    get_cot = remote(cot_in.at[1 - x], cot.at[pl.ds(PART, PART)], ex_send.at[1], ex_recv.at[1], at_x)
+    get_tok.start()
+    get_cot.start()
+
+    core_copies = []
+
+    def to_core(source, target):
+        n = len(core_copies)
+        copy = remote(source, target, core_send.at[n], core_recv.at[n], at_core)
+        copy.start()
+        core_copies.append(copy)
+        return copy
+
+    for row, ref in (
+        (B_QUERY, b_query_in), (B_VALUE, b_value_in), (B_OUT, b_out_in), (FIRST_GAIN, first_gain_in), (FIRST_SHIFT, first_shift_in),
+        (B_DOWN, b_down_in), (SECOND_GAIN, second_gain_in), (SECOND_SHIFT, second_shift_in),
+    ):
+        par[row : row + 1, :] = ref[...].reshape(1, WIDTH)
+    for t in range(4):
+        par[B_UP + t : B_UP + t + 1, :] = b_up_in[WIDTH * t : WIDTH * (t + 1)].reshape(1, WIDTH)
+    vec_mine[0] = jnp.zeros((16, WIDTH), F32)
+    length = lengths_in[0, x]
+    mine, across = 2 * x + core, 2 * (1 - x) + core
+    theirs, theirs_across = 2 * x + 1 - core, 2 * (1 - x) + 1 - core
+
+    def positions(shape, starts):
+        n = lax.broadcasted_iota(jnp.int32, shape, 0)
+        first = starts[-1] * PART
+        for b in range(len(starts) - 2, -1, -1):
+            first = jnp.where(n < PART * (b + 1), starts[b] * PART, first)
+        return first + n % PART
+
+    bias[...] = jnp.where(positions((512, ROWS), (mine, across, theirs, theirs_across)) < length, 0.0, -1e30)
+
+    kv_copies = []
+    for b in range(2):
+        rows = slice(PART * b, PART * (b + 1))
+        if b == 0:
+            loads[0].wait()
+        else:
+            get_tok.wait_recv()
+        for n, s in enumerate((1, 2, 0)):
+            if b == 0:
+                loads[1 + n].wait()
+            part = dot(tok[rows, :], w_qkv[:, WIDTH * s : WIDTH * (s + 1)])
+            if s == 0:
+                part = part + par[B_QUERY : B_QUERY + 1, :]
+            if s == 2:
+                part = part + par[B_VALUE : B_VALUE + 1, :]
+            part = part.astype(BF16)
+            if s == 0:
+                part = part * jnp.asarray(0.125, BF16)
+            held = (q3, k3, v3)[s]
+            for j in range(6):
+                held[j, rows, :] = part[:, 128 * j : 128 * (j + 1)]
+            if s:
+                kv_copies.append(
+                    to_core(held.at[:, pl.ds(PART * b, PART)], held.at[:, pl.ds(ROWS + PART * b, PART)])
+                )
+    tok_t[:, 0:ROWS] = tok[...].T
+    qkv_copies = [to_core(tok_t.at[:, pl.ds(0, ROWS)], tok_t.at[:, pl.ds(ROWS, ROWS)])]
+    for copy in kv_copies:
+        copy.wait_recv()
+
+    low_half = lax.broadcasted_iota(jnp.int32, (ROWS, 128), 1) < 64
+
+    def half_of(pair, h):
+        zeros = jnp.zeros_like(pair)
+        return jnp.where(low_half, pair, zeros) if h == 0 else jnp.where(low_half, zeros, pair)
+
+    def attend(j, _):
+        queries, keys = q3[j], k3[j]
+        values_t = v3[j].T
+        for h in range(2):
+            scores = dot_t(keys, half_of(queries, h)) + bias[...]
+            exponent = jnp.exp(scores - jnp.max(scores, axis=0, keepdims=True))
+            weight = (exponent * (1.0 / jnp.sum(exponent, axis=0, keepdims=True))).astype(BF16)
+            probs[2 * j + h] = weight
+            ctx_t[pl.ds(pl.multiple_of(128 * j + 64 * h, 64), 64), 0:ROWS] = dot(values_t[64 * h : 64 * (h + 1)], weight).astype(BF16)
+        return 0
+
+    lax.fori_loop(0, 6, attend, 0)
+    qkv_copies.append(to_core(ctx_t.at[:, pl.ds(0, ROWS)], ctx_t.at[:, pl.ds(ROWS, ROWS)]))
+
+    loads[5].wait()
+    wide[...] = dot(ctx_t[:, 0:ROWS].T, w_out[...])
+
+    def first_norm(r, _):
+        rows = pl.ds(pl.multiple_of(STEP * r, STEP), STEP)
+        value = tok[rows, :].astype(F32) + wide[rows, :] + par[B_OUT : B_OUT + 1, :]
+        center = value - mean(value)
+        root = lax.rsqrt(mean(center * center) + EPSILON)
+        normed = center * root
+        out = normed * par[FIRST_GAIN : FIRST_GAIN + 1, :] + par[FIRST_SHIFT : FIRST_SHIFT + 1, :]
+        xhat[rows, :] = normed
+        rstd[rows, :] = root
+        hidden[rows, :] = out
+        low[rows, :] = out.astype(BF16)
+        return 0
+
+    lax.fori_loop(0, ROWS // STEP, first_norm, 0)
+    hid_t[:, 0:ROWS] = low[...].T
+    up_copies = [to_core(hid_t.at[:, pl.ds(0, ROWS)], hid_t.at[:, pl.ds(ROWS, ROWS)])]
+
+    for n in range(6, 14):
+        loads[n].wait()
+    total[...] = jnp.zeros_like(total)
+
+    def act_copy(t):
+        return remote(act.at[t, pl.ds(0, ROWS)], act.at[t, pl.ds(ROWS, ROWS)], act_send.at[t], act_recv.at[t], at_core)
+
+    def feed(t, _):
+        wide[...] = dot(low[...], w_up[t])
+
+        def gelu(r, _):
+            rows = pl.ds(pl.multiple_of(STEP * r, STEP), STEP)
+            u = wide[rows, :] + par[pl.ds(B_UP + t, 1), :]
+            phi = 0.5 * (1.0 + lax.erf(u * ROOT_HALF))
+            act[t, rows, :] = (u * phi).astype(BF16)
+            slope[t, rows, :] = phi + u * jnp.exp(-0.5 * u * u) * INV_ROOT_TWO_PI
+            return 0
+
+        lax.fori_loop(0, ROWS // STEP, gelu, 0)
+        act_copy(t).start()
+        total[...] += dot(act[t, 0:ROWS, :], w_down[t])
+        return 0
+
+    lax.fori_loop(0, 4, feed, 0)
+
+    loads[4].wait()
+    get_cot.wait_recv()
+
+    def second_norm(r, carry):
+        rows = pl.ds(pl.multiple_of(STEP * r, STEP), STEP)
+        value = hidden[rows, :] + (total[rows, :] + par[B_DOWN : B_DOWN + 1, :])
+        center = value - mean(value)
+        root = lax.rsqrt(mean(center * center) + EPSILON)
+        normed = center * root
+        n = lax.broadcasted_iota(jnp.int32, (STEP, 1), 0) + STEP * r
+        live = jnp.where(jnp.where(n < PART, mine * PART + n, across * PART + n - PART) < length, 1.0, 0.0)
+        out = (normed * par[SECOND_GAIN : SECOND_GAIN + 1, :] + par[SECOND_SHIFT : SECOND_SHIFT + 1, :]) * live
+        out_rows[rows, :] = out.astype(BF16)
+        grad = cot[rows, :].astype(F32) * live
+        e = grad * par[SECOND_GAIN : SECOND_GAIN + 1, :]
+        d = root * (e - mean(e) - normed * mean(e * normed))
+        dsum[rows, :] = d
+        d_low = d.astype(BF16)
+        low[rows, :] = d_low
+        gain, shift, down = carry
+        return gain + fold(grad * normed), shift + fold(grad), down + fold(d_low.astype(F32))
+
+    zero = jnp.zeros((8, WIDTH), F32)
+    gain, shift, down = lax.fori_loop(0, ROWS // STEP, second_norm, (zero, zero, zero))
+
+    def put(row, partial):
+        vec_mine[0, row : row + 1, :] = jnp.sum(partial, axis=0, keepdims=True)
+
+    put(SECOND_GAIN, gain)
+    put(SECOND_SHIFT, shift)
+    put(B_DOWN, down)
+    out_local = pltpu.make_async_copy(out_rows.at[pl.ds(0, PART)], tokens_out.at[x], load.at[14])
+    out_across = remote(out_rows.at[pl.ds(PART, PART)], tokens_out.at[x], ex_send.at[2], ex_recv.at[2], at_x)
+    out_local.start()
+    out_across.start()
+    dffn_all = low[...].T
+    for j in range(4):
+        dffn_t[j, :, 0:ROWS] = dffn_all[192 * j : 192 * (j + 1), :]
+    down_copies = []
+    for j in (0, 2):
+        there = j + 1 - core
+        down_copies.append(to_core(dffn_t.at[there, :, pl.ds(0, ROWS)], dffn_t.at[there, :, pl.ds(ROWS, ROWS)]))
+
+    def first(m, k):
+        zk = (z + k) % 4
+        if (m, k) in X_FIRST:
+            return remote(sums[m].at[1 - x, zk], in1[m].at[zk], send1.at[m, k], recv1.at[m, k], at_x)
+        return remote(sums[m].at[:, zk, 1 - y], in1[m].at[zk], send1.at[m, k], recv1.at[m, k], at_y)
+
+    def second(m, k):
+        zk = (z + k) % 4
+        if (m, k) in X_FIRST:
+            return remote(sums[m].at[x, zk, 1 - y], in2[m].at[zk], send2.at[m, k], recv2.at[m, k], at_y)
+        return remote(sums[m].at[1 - x, zk, y], in2[m].at[zk], send2.at[m, k], recv2.at[m, k], at_x)
+
+    def third(m, k):
+        zk = (z + k) % 4
+        return remote(sums[m].at[x, zk, y], in3[m].at[k - 1], send3.at[m, k], recv3.at[m, k], at_z[k - 1])
+
+    def add_first(m, k):
+        zk = (z + k) % 4
+        if (m, k) in X_FIRST:
+            sums[m][x, zk] = sums[m][x, zk] + in1[m][zk]
+        else:
+            for b in range(2):
+                sums[m][b, zk, y] = sums[m][b, zk, y] + in1[m][zk, b]
+
+    def add_second(m, k):
+        zk = (z + k) % 4
+        sums[m][x, zk, y] = sums[m][x, zk, y] + in2[m][zk]
+
+    lag = 2
+    done = [0]
+
+    def advance(steps):
+        for step in range(done[0], min(done[0] + steps, len(CHUNKS) + lag)):
+            if step < len(CHUNKS):
+                m, k = CHUNKS[step]
+                first(m, k).wait_recv()
+                add_first(m, k)
+                second(m, k).start()
+            if step >= lag:
+                m, k = CHUNKS[step - lag]
+                second(m, k).wait_recv()
+                add_second(m, k)
+                if k:
+                    third(m, k).start()
+        done[0] += steps
+
+    total[...] = dsum[...]
+
+    def feed_back(t, _):
+        wide[...] = dot_t(low[...], w_down[t])
+
+        def times_slope(r, carry):
+            rows = pl.ds(pl.multiple_of(STEP * r, STEP), STEP)
+            d = (wide[rows, :] * slope[t, rows, :]).astype(BF16)
+            dpre[t, rows, :] = d
+            return carry + fold(d.astype(F32))
+
+        partial = lax.fori_loop(0, ROWS // STEP, times_slope, zero)
+        vec_mine[0, pl.ds(B_UP + t, 1), :] = jnp.sum(partial, axis=0, keepdims=True)
+        total[...] += dot_t(dpre[t, 0:ROWS, :], w_up[t])
+        return 0
+
+    lax.fori_loop(0, 4, feed_back, 0)
+    for j in (0, 2):
+        there = j + 1 - core
+        up_copies.append(to_core(dpre.at[there, pl.ds(0, ROWS)], dpre.at[there, pl.ds(ROWS, ROWS)]))
+
+    for t in range(4):
+        act_copy(t).wait_recv()
+    for copy in down_copies:
+        copy.wait_recv()
+    left = jnp.concatenate([dffn_t[core], dffn_t[2 + core]], axis=0)
+    for t in range(4):
+        part = dot(left, act[t]).astype(BF16)
+        for b in range(2):
+            for h in range(2):
+                sums_0[b, t, h] = part[192 * b : 192 * (b + 1), 384 * h : 384 * (h + 1)]
+    for k in ORDER:
+        first(DOWN, k).start()
+    for copy in up_copies:
+        copy.wait_recv()
+    for b in range(2):
+        for n in range(3):
+            part = dot(hid_t[...], dpre[2 * b + core, :, 256 * n : 256 * (n + 1)]).astype(BF16)
+            sums_1[b, :, :, :, 256 * n : 256 * (n + 1)] = part.reshape(4, 2, 96, 256)
+    for k in ORDER:
+        first(UP, k).start()
+
+    def first_norm_back(r, carry):
+        rows = pl.ds(pl.multiple_of(STEP * r, STEP), STEP)
+        d_hidden, normed = total[rows, :], xhat[rows, :]
+        e = d_hidden * par[FIRST_GAIN : FIRST_GAIN + 1, :]
+        d = rstd[rows, :] * (e - mean(e) - normed * mean(e * normed))
+        dsum[rows, :] = d
+        d_low = d.astype(BF16)
+        low[rows, :] = d_low
+        gain, shift, out = carry
+        return gain + fold(d_hidden * normed), shift + fold(d_hidden), out + fold(d_low.astype(F32))
+
+    gain, shift, out = lax.fori_loop(0, ROWS // STEP, first_norm_back, (zero, zero, zero))
+    put(FIRST_GAIN, gain)
+    put(FIRST_SHIFT, shift)
+    put(B_OUT, out)
+    for j in range(4):
+        dbr[j, 0:ROWS, :] = jnp.concatenate([jnp.zeros((ROWS, 64), BF16), low[:, 192 * j : 192 * (j + 1)]], axis=1)
+    for j in (0, 2):
+        there = j + 1 - core
+        qkv_copies.append(to_core(dbr.at[there, pl.ds(0, ROWS)], dbr.at[there, pl.ds(ROWS, ROWS)]))
+    d_context = dot_t(low[...], w_out[...]).astype(BF16)
+    for j in range(6):
+        dctx3[j] = d_context[:, 128 * j : 128 * (j + 1)]
+
+    def attend_back(j, _):
+        queries, keys, values, d_ctx = q3[j], k3[j], v3[j], dctx3[j]
+        keys_t = keys.T
+        d_keys = jnp.zeros((512, 128), F32)
+        d_values = jnp.zeros((512, 128), F32)
+        for h in range(2):
+            d_head = half_of(d_ctx, h)
+            weight = probs[2 * j + h]
+            d_probs = dot_t(values, d_head)
+            d_values = d_values + dot(weight, d_head)
+            wide_weight = weight.astype(F32)
+            inner = jnp.sum(wide_weight * d_probs, axis=0, keepdims=True)
+            d_scores = (wide_weight * (d_probs - inner)).astype(BF16)
+            d_keys = d_keys + dot(d_scores, half_of(queries, h))
+            dq_t[pl.ds(pl.multiple_of(128 * j + 64 * h, 64), 64), :] = (dot(keys_t[64 * h : 64 * (h + 1)], d_scores) * 0.125).astype(BF16)
+        dkv_own[0, j] = d_keys[0:ROWS]
+        dkv_own[1, j] = d_values[0:ROWS]
+        dkv_send[0, j] = d_keys[ROWS:].astype(BF16)
+        dkv_send[1, j] = d_values[ROWS:].astype(BF16)
+        return 0
+
+    lax.fori_loop(0, 3, attend_back, 0)
+    back_copies = [to_core(dkv_send.at[:, pl.ds(0, 3)], dkv_in.at[:, pl.ds(0, 3)])]
+    lax.fori_loop(3, 6, attend_back, 0)
+    back_copies.append(to_core(dkv_send.at[:, pl.ds(3, 3)], dkv_in.at[:, pl.ds(3, 3)]))
+    d_queries = dq_t[...].T
+    dqkv_flat[:, 0:WIDTH] = d_queries
+    put(B_QUERY, fold(d_queries.astype(F32)))
+    for copy in back_copies:
+        copy.wait_recv()
+    for j in range(6):
+        for s in range(2):
+            d = (dkv_own[s, j] + dkv_in[s, j].astype(F32)).astype(BF16)
+            dqkv_flat[:, WIDTH * (1 + s) + 128 * j : WIDTH * (1 + s) + 128 * (j + 1)] = d
+            if s:
+                vec_mine[0, B_VALUE : B_VALUE + 1, 128 * j : 128 * (j + 1)] = jnp.sum(d.astype(F32), axis=0, keepdims=True)
+    for j in range(4):
+        dqkv[j, 0:ROWS, :] = jnp.concatenate(
+            [dqkv_flat[:, 576 * j : 576 * (j + 1)], jnp.zeros((ROWS, 64), BF16)], axis=1
+        )
+    for j in (0, 2):
+        there = j + 1 - core
+        qkv_copies.append(to_core(dqkv.at[there, pl.ds(0, ROWS)], dqkv.at[there, pl.ds(ROWS, ROWS)]))
+    vec_steps = [
+        remote(vec_mine.at[s], vec_in.at[s], vec_send.at[s], vec_recv.at[s], w) for s, w in enumerate((at_core, at_x, at_y))
+    ]
+    vec_steps[0].start()
+
+    for copy in qkv_copies:
+        copy.wait_recv()
+    for b in range(2):
+        one = dot(tok_t[...], dqkv[2 * b + core])
+        two = dot(ctx_t[...], dbr[2 * b + core])
+        part = jnp.concatenate([one[:, 0:512], one[:, 512:640] + two[:, 0:128], two[:, 128:256]], axis=1).astype(BF16)
+        sums_2[b] = part.reshape(4, 2, 96, WIDTH)
+    for k in ORDER:
+        first(QKV, k).start()
+    vec_steps[0].wait_recv()
+    vec_mine[1] = vec_mine[0] + vec_in[0]
+    vec_steps[1].start()
+    grad_rows[...] = (dsum[...] + dot_t(dqkv_flat[...], w_qkv[...])).astype(BF16)
+    grad_local = pltpu.make_async_copy(grad_rows.at[pl.ds(0, PART)], grad_out.at[x], load.at[15])
+    grad_across = remote(grad_rows.at[pl.ds(PART, PART)], grad_out.at[x], ex_send.at[3], ex_recv.at[3], at_x)
+    grad_local.start()
+    grad_across.start()
+    advance(2)
+    vec_steps[1].wait_recv()
+    vec_mine[2] = vec_mine[1] + vec_in[1]
+    vec_steps[2].start()
+    advance(2)
+    vec_steps[2].wait_recv()
+    vec_mine[3] = vec_mine[2] + vec_in[2]
+    vec_z = [
+        remote(vec_mine.at[3], vec_in.at[3 + z], vec_send.at[2 + k], vec_recv.at[2 + k], at_z[k - 1])
+        for k in (1, 2, 3)
+    ]
+    for copy in vec_z:
+        copy.start()
+    vec_in[3 + z] = vec_mine[3]
+    advance(len(CHUNKS))
+    for copy in vec_z:
+        copy.wait_recv()
+    vec_out[...] = (vec_in[3] + vec_in[4]) + (vec_in[5] + vec_in[6])
+    for m, out in ((DOWN, down_out), (UP, up_out), (QKV, qkv_out)):
+        for k in (1, 2, 3):
+            third(m, k).wait_recv()
+        block = sums[m][x, z, y].astype(F32)
+        for k in range(3):
+            block = block + in3[m][k].astype(F32)
+        out[...] = block
+
+    out_across.wait_recv()
+    grad_across.wait_recv()
+    out_local.wait()
+    grad_local.wait()
+    for copy in [get_tok, get_cot, out_across, grad_across] + core_copies + vec_steps + vec_z:
+        copy.wait_send()
+    for t in range(4):
+        act_copy(t).wait_send()
+    for m, k in CHUNKS:
+        first(m, k).wait_send()
+        second(m, k).wait_send()
+        if k:
+            third(m, k).wait_send()
+
+
+def local(
+    tokens, lengths, cotangent, w_qkv, b_query, b_value, w_out, b_out, first_gain, first_shift, w_up, b_up, w_down, b_down,
+    second_gain, second_shift,
+):
+    vmem = pl.BlockSpec(memory_space=pltpu.VMEM)
+    hbm = pl.BlockSpec(memory_space=pl.ANY)
+    dma = pltpu.SemaphoreType.DMA
+    B, W = pltpu.VMEM, WIDTH
+    scratch = [
+        B((W, 3 * W), BF16), B((W, W), BF16), B((4, W, W), BF16), B((4, W, W), BF16), B((16, W), F32),
+        B((ROWS, W), BF16), B((ROWS, W), BF16),
+        B((6, ROWS, 128), BF16), B((6, 512, 128), BF16), B((6, 512, 128), BF16),
+        B((512, ROWS), F32), B((12, 512, ROWS), BF16),
+        B((ROWS, W), F32), B((ROWS, W), F32), B((ROWS, 1), F32), B((ROWS, W), BF16),
+        B((4, ROWS, W), F32), B((ROWS, W), F32), B((ROWS, W), F32), B((ROWS, W), F32),
+        B((6, ROWS, 128), BF16), B((2, 6, ROWS, 128), F32), B((2, 6, ROWS, 128), BF16), B((2, 6, ROWS, 128), BF16),
+        B((W, ROWS), BF16), B((ROWS, 3 * W), BF16), B((ROWS, W), BF16), B((ROWS, W), BF16),
+        B((4, 512, W), BF16), B((4, 512, W), BF16), B((4, 192, 512), BF16),
+        B((W, 512), BF16), B((W, 512), BF16), B((W, 512), BF16), B((4, 512, 640), BF16), B((4, 512, 256), BF16),
+    ]
+    scratch += [B((2, 4, 2) + block, BF16) for block in BLOCKS]
+    scratch += [B((4, 2) + block, BF16) for block in BLOCKS]
+    scratch += [B((4,) + block, BF16) for block in BLOCKS]
+    scratch += [B((3,) + block, BF16) for block in BLOCKS]
+    scratch += [B((4, 16, W), F32), B((7, 16, W), F32)]
+    scratch += [dma((16,)), dma((4,)), dma((4,)), dma((24,)), dma((24,)), dma((4,)), dma((4,))]
+    scratch += [dma((3, 4))] * 6 + [dma((6,)), dma((6,))]
+    out_tokens, grad_tokens, down, up, joined, vectors = pl.pallas_call(
+        layer_kernel,
+        name="layer",
+        out_shape=(
+            jax.ShapeDtypeStruct(tokens.shape, BF16),
+            jax.ShapeDtypeStruct(tokens.shape, BF16),
+            jax.ShapeDtypeStruct(BLOCKS[DOWN], F32),
+            jax.ShapeDtypeStruct(BLOCKS[UP], F32),
+            jax.ShapeDtypeStruct(BLOCKS[QKV], F32),
+            jax.ShapeDtypeStruct((16, W), F32),
+        ),
+        in_specs=[hbm, pl.BlockSpec(memory_space=pltpu.SMEM)] + [hbm] * 5 + [vmem] * 9,
+        out_specs=(hbm, hbm) + (vmem,) * 4,
+        scratch_shapes=scratch,
+        compiler_params=pltpu.CompilerParams(
+            collective_id=1, has_side_effects=True, vmem_limit_bytes=63 * 1024 * 1024
+        ),
+    )(
+        tokens, lengths, cotangent, w_qkv, w_out, w_up, w_down,
+        b_query, b_value, b_out, first_gain, first_shift, b_up, b_down, second_gain, second_shift,
+    )
+    return (
+        out_tokens, grad_tokens, joined[:, :576], joined[:, 576:], up, down.T,
+        vectors[B_QUERY], vectors[B_VALUE], vectors[B_OUT], vectors[FIRST_GAIN], vectors[FIRST_SHIFT],
+        vectors[B_UP : B_UP + 4].reshape(-1), vectors[B_DOWN], vectors[SECOND_GAIN], vectors[SECOND_SHIFT],
+    )
+
+
 def solution(mesh):
     in_specs = (
         P("dp", "seq", None),
@@ -283,4 +827,5 @@
         P(),
         P(),
     )
-    return jax.shard_map(local, mesh=mesh, in_specs=in_specs, out_specs=out_specs, check_vma=False)
+    return jax.shard_map(
+        local if dict(mesh.shape) == {"dp": 8, "seq": 4} else local_any, mesh=mesh, in_specs=in_specs, out_specs=out_specs, check_vma=False)

time: 760 us -> 147 us (0.19)
  waiting for transfers between devices: 504 us -> 0 us
  Pallas kernels: 0 us -> 133 us
  blocking collectives: 65.6 us -> 0 us
  matrix products: 63.9 us -> 0 us
  local copies, waits for them, and re-layouts: 70.2 us -> 13.3 us
  other arithmetic: 25.5 us -> 0 us
  between operations: 14.6 us -> 0.67 us
  starting transfers between devices: 13.2 us -> 0 us
    reduce_scatter x5 -> x0, waiting for transfers between devices: 347 us -> none  [the longest x1 164 us: local(): lax.psum_scatter(matrices[3], 'dp', scatter_dimension=0, tiled=True)]
    pallas_call x0 -> x1, Pallas kernels: none -> 133 us  [local(): pl.pallas_call(layer_kernel, name='layer', out_shape=(jax.ShapeDtypeStruc...]
    unnamed x11 -> x0, waiting for transfers between devices: 132 us -> none
    dot_general x26 -> x0, matrix products: 63.9 us -> none  [the longest x4 21.7 us: contract_rows(): lax.dot_general(left, right, (((0,), (0,)), ((), ())), preferred_element_...]
    psum x1 -> x0, blocking collectives: 41.1 us -> none  [local(): lax.psum((grad_b_query, grad_b_value, grad_b_out, grad_first_gain, grad_f...]
    all_to_all x3 -> x0, waiting for transfers between devices: 25.3 us -> none  [the longest x1 15.8 us: local(): lax.all_to_all(mixed.astype(jnp.bfloat16).reshape(seq_count, part_len, 3,...]
    all_to_all x1 -> x0, blocking collectives: 24.5 us -> none  [local(): lax.all_to_all(d_qkv_heads, 'seq', split_axis=1, concat_axis=3, tiled=True)]
    reshape x7 -> x1, local copies, waits for them, and re-layouts: 23.4 us -> 0.61 us  [local(): vectors[B_UP:B_UP + 4].reshape(-1)]
  transfers between devices with their start and end apart: 11 -> 0, of which waited for: 8 -> 0; matrix products, arithmetic and copies ran while one was open for 12% -> 0% of each run, Pallas kernels for 0% -> 0%
where the time goes in v2:
time: 147 us
  Pallas kernels  133 us (90%)
  local copies, waits for them, and re-layouts  13.3 us (9%)
    pallas_call x1, Pallas kernels, local(): pl.pallas_call(layer_kernel, name='layer', out_shape=(jax.ShapeDtypeStruc...  133 us
    unnamed x4, local copies, waits for them, and re-layouts  6.92 us

profile of v2, /device:TPU:0, one launch (start us, length us, event | category | flops | bytes accessed | tf_op | source)
XLA Modules:
  0.0 146.9 jit_solution(14799549132849811669)
XLA Ops:
  0.7 133.0 %layer.1 = (bf16[2,128,768]{2,1,0:T(8,128)(2,1)}, bf16[2,128,768]{2,1,0:T(8,128)(2,1)}, f32[192,384]{1,0:T(8,128)}, f32[96,768]{1,0:T(8,128)}, f32[96,768]{1,0:T(8,128)}, /*index=5*/f32[16,768]{1,0:T(8,128)}) custom-call(bf16[2,128,768]{2,1,0:T(8,128)(2,1)} %tokens_in.1, s32[1,2]{1,0:T(1,128)} %lengths_in.1, bf16[2,128,768]{2,1,0:T(8,128)(2,1)} %cot_in.1, ...), custom_call_target="tpu_custom_call" | custom-call | tf_op jit(solution)/shard_map/layer/pallas_call | solution.py:766
  133.6 1.7 %slice.33 = f32[96,576]{1,0:T(8,128)} slice(f32[96,768]{1,0:T(8,128)} %get-tuple-element.23), slice={[0:96], [0:576]} | slice | bytes 442368 | tf_op jit(solution)/shard_map/slice | solution.py:788
  135.3 1.6 %slice.34 = f32[96,192]{1,0:T(8,128)} slice(f32[96,768]{1,0:T(8,128)} %get-tuple-element.23), slice={[0:96], [576:768]} | slice | bytes 147456 | tf_op jit(solution)/shard_map/slice | solution.py:788
  136.9 1.7 %slice_reduce_fusion = (f32[768]{0:T(1024)}, f32[768]{0:T(1024)}, f32[768]{0:T(1024)}, f32[768]{0:T(1024)}, f32[768]{0:T(1024)}, /*index=5*/f32[768]{0:T(1024)}, f32[768]{0:T(1024)}, f32[768]{0:T(1024)}) fusion(f32[16,768]{1,0:T(8,128)} %get-tuple-element.26), kind=kLoop, calls=%fused_computation | loop fusion | bytes 49152 | tf_op jit(solution)/shard_map/slice | solution.py:790
  138.6 0.7 slice.40
  139.4 0.6 reshape.33
  140.0 1.8 %copy.35 = bf16[2,128,768]{2,1,0:T(8,128)(2,1)} copy(bf16[2,128,768]{2,1,0:T(8,128)(2,1)} %get-tuple-element.50) | data formatting | bytes 786432
  141.8 1.8 %copy.36 = bf16[2,128,768]{2,1,0:T(8,128)(2,1)} copy(bf16[2,128,768]{2,1,0:T(8,128)(2,1)} %get-tuple-element.51) | data formatting | bytes 786432
  143.5 1.7 %copy.37 = f32[96,768]{1,0:T(8,128)} copy(f32[96,768]{1,0:T(8,128)} %get-tuple-element.54) | data formatting | bytes 589824
  145.2 1.7 %copy.38 = f32[384,192]{0,1:T(8,128)} copy(f32[384,192]{0,1:T(8,128)} %bitcast.1) | data formatting | bytes 589824

commit v3 on v2

--- a/solution.py
+++ b/solution.py
@@ -256,17 +256,33 @@
 
 
 DOWN, UP, QKV = 0, 1, 2
-ORDER = (1, 2, 3, 0)
-CHUNKS = tuple((m, k) for k in ORDER for m in (DOWN, UP)) + tuple((QKV, k) for k in ORDER)
-X_FIRST = {(UP, 0), (UP, 1), (UP, 2), (UP, 3), (QKV, 2), (QKV, 0)}
 BLOCKS = ((192, 384), (96, 768), (96, 768))
+PLAN = (
+    ((0, 0, 2), (0, 0, 1),),
+    (),
+    (),
+    (),
+    ((0, 0, 3), (0, 0, 0),),
+    (),
+    ((1, 0, 1), (1, 0, 2),),
+    (),
+    (),
+    ((0, 1, 2), (0, 1, 1),),
+    ((1, 0, 0), (1, 0, 3),),
+    ((2, 0, 1), (2, 0, 2),),
+    (),
+    ((1, 1, 1), (1, 1, 2),),
+    ((2, 0, 0), (0, 1, 3), (2, 0, 3), (2, 1, 1), (1, 1, 3), (0, 1, 0), (2, 1, 2), (2, 1, 3), (0, 2, 2), (0, 2, 1), (1, 1, 0), (1, 2, 1), (1, 2, 2), (0, 2, 3), (2, 1, 0), (0, 2, 0), (2, 2, 1), (2, 2, 2), (1, 2, 3), (1, 2, 0), (2, 2, 3), (2, 2, 0),),
+)
+X_FIRST = {(0, 0), (0, 1), (1, 1), (2, 0), (2, 1)}
+ORDER_D = (2, 1, 3, 0)
 
 B_QUERY, B_VALUE, B_OUT, FIRST_GAIN, FIRST_SHIFT, B_DOWN, SECOND_GAIN, SECOND_SHIFT, B_UP = range(9)
 
 ROWS = 256
 PART = 128
 WIDTH = 768
-STEP = 32
+STEP = 128
 
 
 def place():
@@ -315,7 +331,8 @@
     sums_0, sums_1, sums_2, in1_0, in1_1, in1_2, in2_0, in2_1, in2_2, in3_0, in3_1, in3_2,
     vec_mine, vec_in,
     load, ex_send, ex_recv, core_send, core_recv, act_send, act_recv,
-    send1, recv1, send2, recv2, send3, recv3, vec_send, vec_recv,
+    send1, recv1, send2, recv2, send3, recv3, vec_send, vec_recv, vec_load,
+    held_0, held_1, held_2, held_3, held_4, held_5, held_6, held_7, held_8,
 ):
     z, y, x, core = place()
     sums, in1, in2, in3 = (sums_0, sums_1, sums_2), (in1_0, in1_1, in1_2), (in2_0, in2_1, in2_2), (in3_0, in3_1, in3_2)
@@ -337,7 +354,18 @@
         loads.append(pltpu.make_async_copy(w_up_in.at[:, pl.ds(WIDTH * t, WIDTH)], w_up.at[t], load.at[6 + t]))
     for t in range(4):
         loads.append(pltpu.make_async_copy(w_down_in.at[pl.ds(WIDTH * t, WIDTH)], w_down.at[t], load.at[10 + t]))
-    for copy in loads:
+    for copy in loads[0:4]:
+        copy.start()
+
+    vec_refs = {
+        B_QUERY: (b_query_in, held_0), B_VALUE: (b_value_in, held_1), B_OUT: (b_out_in, held_2), FIRST_GAIN: (first_gain_in, held_3),
+        FIRST_SHIFT: (first_shift_in, held_4), B_DOWN: (b_down_in, held_5), SECOND_GAIN: (second_gain_in, held_6),
+        SECOND_SHIFT: (second_shift_in, held_7), B_UP: (b_up_in, held_8),
+    }
+    vec_loads = [
+        pltpu.make_async_copy(source, held, vec_load.at[n]) for n, (source, held) in enumerate(vec_refs.values())
+    ]
+    for copy in vec_loads:
         copy.start()
 
     barrier = pltpu.get_barrier_semaphore()
@@ -348,7 +376,6 @@
     get_tok = remote(tokens_in.at[1 - x], tok.at[pl.ds(PART, PART)], ex_send.at[0], ex_recv.at[0], at_x)
     get_cot = remote(cot_in.at[1 - x], cot.at[pl.ds(PART, PART)], ex_send.at[1], ex_recv.at[1], at_x)
     get_tok.start()
-    get_cot.start()
 
     core_copies = []
 
@@ -359,13 +386,14 @@
         core_copies.append(copy)
         return copy
 
-    for row, ref in (
-        (B_QUERY, b_query_in), (B_VALUE, b_value_in), (B_OUT, b_out_in), (FIRST_GAIN, first_gain_in), (FIRST_SHIFT, first_shift_in),
-        (B_DOWN, b_down_in), (SECOND_GAIN, second_gain_in), (SECOND_SHIFT, second_shift_in),
-    ):
-        par[row : row + 1, :] = ref[...].reshape(1, WIDTH)
-    for t in range(4):
-        par[B_UP + t : B_UP + t + 1, :] = b_up_in[WIDTH * t : WIDTH * (t + 1)].reshape(1, WIDTH)
+    for copy in vec_loads:
+        copy.wait()
+    for row, (_, held) in vec_refs.items():
+        if row == B_UP:
+            for t in range(4):
+                par[B_UP + t : B_UP + t + 1, :] = held[WIDTH * t : WIDTH * (t + 1)].reshape(1, WIDTH)
+        else:
+            par[row : row + 1, :] = held[...].reshape(1, WIDTH)
     vec_mine[0] = jnp.zeros((16, WIDTH), F32)
     length = lengths_in[0, x]
     mine, across = 2 * x + core, 2 * (1 - x) + core
@@ -387,6 +415,7 @@
             loads[0].wait()
         else:
             get_tok.wait_recv()
+            get_cot.start()
         for n, s in enumerate((1, 2, 0)):
             if b == 0:
                 loads[1 + n].wait()
@@ -405,6 +434,11 @@
                 kv_copies.append(
                     to_core(held.at[:, pl.ds(PART * b, PART)], held.at[:, pl.ds(ROWS + PART * b, PART)])
                 )
+        if b == 0:
+            for copy in loads[5:14]:
+                copy.start()
+        else:
+            loads[4].start()
     tok_t[:, 0:ROWS] = tok[...].T
     qkv_copies = [to_core(tok_t.at[:, pl.ds(0, ROWS)], tok_t.at[:, pl.ds(ROWS, ROWS)])]
     for copy in kv_copies:
@@ -427,7 +461,7 @@
             ctx_t[pl.ds(pl.multiple_of(128 * j + 64 * h, 64), 64), 0:ROWS] = dot(values_t[64 * h : 64 * (h + 1)], weight).astype(BF16)
         return 0
 
-    lax.fori_loop(0, 6, attend, 0)
+    lax.fori_loop(0, 6, attend, 0, unroll=True)
     qkv_copies.append(to_core(ctx_t.at[:, pl.ds(0, ROWS)], ctx_t.at[:, pl.ds(ROWS, ROWS)]))
 
     loads[5].wait()
@@ -457,23 +491,14 @@
     def act_copy(t):
         return remote(act.at[t, pl.ds(0, ROWS)], act.at[t, pl.ds(ROWS, ROWS)], act_send.at[t], act_recv.at[t], at_core)
 
-    def feed(t, _):
-        wide[...] = dot(low[...], w_up[t])
-
-        def gelu(r, _):
-            rows = pl.ds(pl.multiple_of(STEP * r, STEP), STEP)
-            u = wide[rows, :] + par[pl.ds(B_UP + t, 1), :]
-            phi = 0.5 * (1.0 + lax.erf(u * ROOT_HALF))
-            act[t, rows, :] = (u * phi).astype(BF16)
-            slope[t, rows, :] = phi + u * jnp.exp(-0.5 * u * u) * INV_ROOT_TWO_PI
-            return 0
-
-        lax.fori_loop(0, ROWS // STEP, gelu, 0)
+    for t in range(4):
+        u = dot(low[...], w_up[t]) + par[B_UP + t : B_UP + t + 1, :]
+        phi = 0.5 * (1.0 + lax.erf(u * ROOT_HALF))
+        active = (u * phi).astype(BF16)
+        act[t, 0:ROWS, :] = active
+        slope[t] = phi + u * jnp.exp(-0.5 * u * u) * INV_ROOT_TWO_PI
         act_copy(t).start()
-        total[...] += dot(act[t, 0:ROWS, :], w_down[t])
-        return 0
-
-    lax.fori_loop(0, 4, feed, 0)
+        total[...] += dot(active, w_down[t])
 
     loads[4].wait()
     get_cot.wait_recv()
@@ -509,7 +534,6 @@
     out_local = pltpu.make_async_copy(out_rows.at[pl.ds(0, PART)], tokens_out.at[x], load.at[14])
     out_across = remote(out_rows.at[pl.ds(PART, PART)], tokens_out.at[x], ex_send.at[2], ex_recv.at[2], at_x)
     out_local.start()
-    out_across.start()
     dffn_all = low[...].T
     for j in range(4):
         dffn_t[j, :, 0:ROWS] = dffn_all[192 * j : 192 * (j + 1), :]
@@ -546,43 +570,31 @@
         zk = (z + k) % 4
         sums[m][x, zk, y] = sums[m][x, zk, y] + in2[m][zk]
 
-    lag = 2
-    done = [0]
-
-    def advance(steps):
-        for step in range(done[0], min(done[0] + steps, len(CHUNKS) + lag)):
-            if step < len(CHUNKS):
-                m, k = CHUNKS[step]
+    def at(point):
+        for step, m, k in PLAN[point]:
+            if step == 0:
+                first(m, k).start()
+            elif step == 1:
                 first(m, k).wait_recv()
                 add_first(m, k)
                 second(m, k).start()
-            if step >= lag:
-                m, k = CHUNKS[step - lag]
+            else:
                 second(m, k).wait_recv()
                 add_second(m, k)
                 if k:
                     third(m, k).start()
-        done[0] += steps
 
     total[...] = dsum[...]
 
-    def feed_back(t, _):
-        wide[...] = dot_t(low[...], w_down[t])
-
-        def times_slope(r, carry):
-            rows = pl.ds(pl.multiple_of(STEP * r, STEP), STEP)
-            d = (wide[rows, :] * slope[t, rows, :]).astype(BF16)
-            dpre[t, rows, :] = d
-            return carry + fold(d.astype(F32))
-
-        partial = lax.fori_loop(0, ROWS // STEP, times_slope, zero)
-        vec_mine[0, pl.ds(B_UP + t, 1), :] = jnp.sum(partial, axis=0, keepdims=True)
-        total[...] += dot_t(dpre[t, 0:ROWS, :], w_up[t])
-        return 0
-
-    lax.fori_loop(0, 4, feed_back, 0)
+    def feed_back(t):
+        d_pre = (dot_t(low[...], w_down[t]) * slope[t]).astype(BF16)
+        dpre[t, 0:ROWS, :] = d_pre
+        vec_mine[0, pl.ds(B_UP + t, 1), :] = jnp.sum(fold(d_pre.astype(F32)), axis=0, keepdims=True)
+        total[...] += dot_t(d_pre, w_up[t])
+
     for j in (0, 2):
         there = j + 1 - core
+        feed_back(there)
         up_copies.append(to_core(dpre.at[there, pl.ds(0, ROWS)], dpre.at[there, pl.ds(ROWS, ROWS)]))
 
     for t in range(4):
@@ -590,21 +602,24 @@
     for copy in down_copies:
         copy.wait_recv()
     left = jnp.concatenate([dffn_t[core], dffn_t[2 + core]], axis=0)
-    for t in range(4):
+    for k in ORDER_D:
+        t = (z + k) % 4
         part = dot(left, act[t]).astype(BF16)
         for b in range(2):
             for h in range(2):
                 sums_0[b, t, h] = part[192 * b : 192 * (b + 1), 384 * h : 384 * (h + 1)]
-    for k in ORDER:
-        first(DOWN, k).start()
+        if (0, DOWN, k) in PLAN[0]:
+            first(DOWN, k).start()
+    for n, j in enumerate((0, 2)):
+        feed_back(j + core)
+        at(1 + n)
     for copy in up_copies:
         copy.wait_recv()
     for b in range(2):
         for n in range(3):
             part = dot(hid_t[...], dpre[2 * b + core, :, 256 * n : 256 * (n + 1)]).astype(BF16)
             sums_1[b, :, :, :, 256 * n : 256 * (n + 1)] = part.reshape(4, 2, 96, 256)
-    for k in ORDER:
-        first(UP, k).start()
+    at(3)
 
     def first_norm_back(r, carry):
         rows = pl.ds(pl.multiple_of(STEP * r, STEP), STEP)
@@ -629,6 +644,8 @@
     d_context = dot_t(low[...], w_out[...]).astype(BF16)
     for j in range(6):
         dctx3[j] = d_context[:, 128 * j : 128 * (j + 1)]
+
+    at(4)
 
     def attend_back(j, _):
         queries, keys, values, d_ctx = q3[j], k3[j], v3[j], dctx3[j]
@@ -651,15 +668,19 @@
         dkv_send[1, j] = d_values[ROWS:].astype(BF16)
         return 0
 
-    lax.fori_loop(0, 3, attend_back, 0)
+    lax.fori_loop(0, 3, attend_back, 0, unroll=True)
     back_copies = [to_core(dkv_send.at[:, pl.ds(0, 3)], dkv_in.at[:, pl.ds(0, 3)])]
-    lax.fori_loop(3, 6, attend_back, 0)
+    at(5)
+    lax.fori_loop(3, 6, attend_back, 0, unroll=True)
     back_copies.append(to_core(dkv_send.at[:, pl.ds(3, 3)], dkv_in.at[:, pl.ds(3, 3)]))
+    at(6)
     d_queries = dq_t[...].T
     dqkv_flat[:, 0:WIDTH] = d_queries
     put(B_QUERY, fold(d_queries.astype(F32)))
+    at(7)
     for copy in back_copies:
         copy.wait_recv()
+    at(8)
     for j in range(6):
         for s in range(2):
             d = (dkv_own[s, j] + dkv_in[s, j].astype(F32)).astype(BF16)
@@ -677,16 +698,17 @@
         remote(vec_mine.at[s], vec_in.at[s], vec_send.at[s], vec_recv.at[s], w) for s, w in enumerate((at_core, at_x, at_y))
     ]
     vec_steps[0].start()
+    at(9)
 
     for copy in qkv_copies:
         copy.wait_recv()
+    at(10)
     for b in range(2):
         one = dot(tok_t[...], dqkv[2 * b + core])
         two = dot(ctx_t[...], dbr[2 * b + core])
         part = jnp.concatenate([one[:, 0:512], one[:, 512:640] + two[:, 0:128], two[:, 128:256]], axis=1).astype(BF16)
         sums_2[b] = part.reshape(4, 2, 96, WIDTH)
-    for k in ORDER:
-        first(QKV, k).start()
+    at(11)
     vec_steps[0].wait_recv()
     vec_mine[1] = vec_mine[0] + vec_in[0]
     vec_steps[1].start()
@@ -695,11 +717,12 @@
     grad_across = remote(grad_rows.at[pl.ds(PART, PART)], grad_out.at[x], ex_send.at[3], ex_recv.at[3], at_x)
     grad_local.start()
     grad_across.start()
-    advance(2)
+    out_across.start()
+    at(12)
     vec_steps[1].wait_recv()
     vec_mine[2] = vec_mine[1] + vec_in[1]
     vec_steps[2].start()
-    advance(2)
+    at(13)
     vec_steps[2].wait_recv()
     vec_mine[3] = vec_mine[2] + vec_in[2]
     vec_z = [
@@ -709,7 +732,7 @@
     for copy in vec_z:
         copy.start()
     vec_in[3 + z] = vec_mine[3]
-    advance(len(CHUNKS))
+    at(14)
     for copy in vec_z:
         copy.wait_recv()
     vec_out[...] = (vec_in[3] + vec_in[4]) + (vec_in[5] + vec_in[6])
@@ -729,11 +752,46 @@
         copy.wait_send()
     for t in range(4):
         act_copy(t).wait_send()
-    for m, k in CHUNKS:
-        first(m, k).wait_send()
-        second(m, k).wait_send()
-        if k:
-            third(m, k).wait_send()
+    for m in (DOWN, UP, QKV):
+        for k in range(4):
+            first(m, k).wait_send()
+            second(m, k).wait_send()
+            if k:
+                third(m, k).wait_send()
+
+
+def finish_kernel(
+    tokens_in, grad_in, down_in, up_in, joined_in, vec_in,
+    tokens_out, grad_out, qkv_out, out_out, up_out, down_out,
+    b_query, b_value, b_out, first_gain, first_shift, b_up, b_down, second_gain, second_shift,
+):
+    tokens_out[...] = tokens_in[...]
+    grad_out[...] = grad_in[...]
+    up_out[...] = up_in[...]
+    qkv_out[...] = joined_in[:, 0:576]
+    out_out[...] = joined_in[:, 576:WIDTH]
+    down_out[...] = down_in[...]
+    for row, ref in (
+        (B_QUERY, b_query), (B_VALUE, b_value), (B_OUT, b_out), (FIRST_GAIN, first_gain), (FIRST_SHIFT, first_shift),
+        (B_DOWN, b_down), (SECOND_GAIN, second_gain), (SECOND_SHIFT, second_shift),
+    ):
+        ref[...] = vec_in[row, :]
+    for t in range(4):
+        b_up[WIDTH * t : WIDTH * (t + 1)] = vec_in[B_UP + t, :]
+
+
+def finish(out_tokens, grad_tokens, down, up, joined, vectors):
+    vmem = pl.BlockSpec(memory_space=pltpu.VMEM)
+    W = WIDTH
+    shapes = [out_tokens.shape] * 2 + [(96, 576), (96, 192), up.shape, down.shape] + [(W,)] * 5 + [(4 * W,)] + [(W,)] * 3
+    outs = pl.pallas_call(
+        finish_kernel,
+        name="finish",
+        out_shape=tuple(jax.ShapeDtypeStruct(s, BF16 if n < 2 else F32) for n, s in enumerate(shapes)),
+        in_specs=[vmem] * 6,
+        out_specs=(vmem,) * 15,
+    )(out_tokens, grad_tokens, down, up, joined, vectors)
+    return outs[:5] + (outs[5].T,) + outs[6:]
 
 
 def local(
@@ -762,8 +820,8 @@
     scratch += [B((3,) + block, BF16) for block in BLOCKS]
     scratch += [B((4, 16, W), F32), B((7, 16, W), F32)]
     scratch += [dma((16,)), dma((4,)), dma((4,)), dma((24,)), dma((24,)), dma((4,)), dma((4,))]
-    scratch += [dma((3, 4))] * 6 + [dma((6,)), dma((6,))]
-    out_tokens, grad_tokens, down, up, joined, vectors = pl.pallas_call(
+    scratch += [dma((3, 4))] * 6 + [dma((6,)), dma((6,)), dma((9,))] + [B((W,), F32)] * 8 + [B((4 * W,), F32)]
+    results = pl.pallas_call(
         layer_kernel,
         name="layer",
         out_shape=(
@@ -774,7 +832,7 @@
             jax.ShapeDtypeStruct(BLOCKS[QKV], F32),
             jax.ShapeDtypeStruct((16, W), F32),
         ),
-        in_specs=[hbm, pl.BlockSpec(memory_space=pltpu.SMEM)] + [hbm] * 5 + [vmem] * 9,
+        in_specs=[hbm, pl.BlockSpec(memory_space=pltpu.SMEM)] + [hbm] * 14,
         out_specs=(hbm, hbm) + (vmem,) * 4,
         scratch_shapes=scratch,
         compiler_params=pltpu.CompilerParams(
@@ -784,11 +842,7 @@
         tokens, lengths, cotangent, w_qkv, w_out, w_up, w_down,
         b_query, b_value, b_out, first_gain, first_shift, b_up, b_down, second_gain, second_shift,
     )
-    return (
-        out_tokens, grad_tokens, joined[:, :576], joined[:, 576:], up, down.T,
-        vectors[B_QUERY], vectors[B_VALUE], vectors[B_OUT], vectors[FIRST_GAIN], vectors[FIRST_SHIFT],
-        vectors[B_UP : B_UP + 4].reshape(-1), vectors[B_DOWN], vectors[SECOND_GAIN], vectors[SECOND_SHIFT],
-    )
+    return finish(*results)
 
 
 def solution(mesh):

time: 147 us -> 108 us (0.73)
  Pallas kernels: 133 us -> 106 us
  local copies, waits for them, and re-layouts: 13.3 us -> 0 us
    pallas_call x1, Pallas kernels: 133 us -> 104 us  [local(): pl.pallas_call(layer_kernel, name='layer', out_shape=(jax.ShapeDtypeStruc...]
    unnamed x4 -> x0, local copies, waits for them, and re-layouts: 6.92 us -> none
    slice x4 -> x0, local copies, waits for them, and re-layouts: 5.73 us -> none  [the longest x1 1.71 us: local(): vectors[SECOND_SHIFT]]
    pallas_call x0 -> x1, Pallas kernels: none -> 2.63 us  [finish(): pl.pallas_call(finish_kernel, name='finish', out_shape=tuple((jax.ShapeDt...]
where the time goes in v3:
time: 108 us; the launch traced here: 107 us
  Pallas kernels  106 us (98%)
    pallas_call x1, Pallas kernels, local(): pl.pallas_call(layer_kernel, name='layer', out_shape=(jax.ShapeDtypeStruc...  104 us
    pallas_call x1, Pallas kernels, finish(): pl.pallas_call(finish_kernel, name='finish', out_shape=tuple((jax.ShapeDt...  2.63 us

profile of v3, /device:TPU:0, one launch (start us, length us, event | category | flops | bytes accessed | tf_op | source)
XLA Modules:
  0.0 107.3 jit_solution(3036077719046031287)
XLA Ops:
  0.7 103.9 %layer.1 = (bf16[2,128,768]{2,1,0:T(8,128)(2,1)}, bf16[2,128,768]{2,1,0:T(8,128)(2,1)}, f32[192,384]{1,0:T(8,128)}, f32[96,768]{1,0:T(8,128)}, f32[96,768]{1,0:T(8,128)}, /*index=5*/f32[16,768]{1,0:T(8,128)}) custom-call(bf16[2,128,768]{2,1,0:T(8,128)(2,1)} %tokens_in.1, s32[1,2]{1,0:T(1,128)} %lengths_in.1, bf16[2,128,768]{2,1,0:T(8,128)(2,1)} %cot_in.1, ...), custom_call_target="tpu_custom_call" | custom-call | tf_op jit(solution)/shard_map/layer/pallas_call | solution.py:824
  104.5 2.6 %finish.1 = (bf16[2,128,768]{2,1,0:T(8,128)(2,1)}, bf16[2,128,768]{2,1,0:T(8,128)(2,1)}, f32[96,576]{1,0:T(8,128)}, f32[96,192]{1,0:T(8,128)}, f32[96,768]{1,0:T...) custom-call(bf16[2,128,768]{2,1,0:T(8,128)(2,1)} %get-tuple-element., ...), custom_call_target="tpu_custom_call" | custom-call | tf_op jit(solution)/shard_map/finish/pallas_call | solution.py:787

commit v4 on v3

--- a/solution.py
+++ b/solution.py
@@ -255,31 +255,33 @@
     )
 
 
-DOWN, UP, QKV = 0, 1, 2
-BLOCKS = ((192, 384), (96, 768), (96, 768))
+DOWN, UP, QKV, DOWN_Z = 0, 1, 2, 3
+BLOCKS = ((96, 384), (96, 768), (96, 768), (96, 384))
 PLAN = (
-    ((0, 0, 2), (0, 0, 1),),
+    ((0, 0, 3), (0, 0, 1), (0, 0, 2),),
     (),
+    ((0, 0, 0),),
+    ((0, 1, 3),),
+    ((0, 1, 1), (0, 1, 2),),
+    ((1, 0, 3), (1, 0, 1), (1, 3, 0),),
+    ((1, 0, 2),),
     (),
+    ((1, 0, 0), (1, 1, 3),),
     (),
-    ((0, 0, 3), (0, 0, 0),),
-    (),
-    ((1, 0, 1), (1, 0, 2),),
-    (),
-    (),
-    ((0, 1, 2), (0, 1, 1),),
-    ((1, 0, 0), (1, 0, 3),),
-    ((2, 0, 1), (2, 0, 2),),
-    (),
-    ((1, 1, 1), (1, 1, 2),),
-    ((2, 0, 0), (0, 1, 3), (2, 0, 3), (2, 1, 1), (1, 1, 3), (0, 1, 0), (2, 1, 2), (2, 1, 3), (0, 2, 2), (0, 2, 1), (1, 1, 0), (1, 2, 1), (1, 2, 2), (0, 2, 3), (2, 1, 0), (0, 2, 0), (2, 2, 1), (2, 2, 2), (1, 2, 3), (1, 2, 0), (2, 2, 3), (2, 2, 0),),
+    ((0, 1, 0),),
+    ((0, 2, 3),),
+    ((1, 1, 1), (1, 1, 2), (2, 0, 1), (2, 0, 3), (2, 3, 0),),
+    ((2, 1, 3), (2, 0, 0),),
+    ((2, 0, 2), (0, 2, 1), (1, 1, 0),),
+    ((1, 2, 3), (2, 1, 2), (1, 2, 1), (0, 2, 2), (2, 1, 1), (2, 2, 3), (0, 2, 0), (3, 3, 0), (2, 1, 0), (1, 2, 2), (2, 2, 1), (2, 2, 2), (1, 2, 0), (4, 3, 0), (2, 2, 0),),
 )
-X_FIRST = {(0, 0), (0, 1), (1, 1), (2, 0), (2, 1)}
-ORDER_D = (2, 1, 3, 0)
+X_FIRST = {(0, 1), (1, 2), (1, 3), (2, 3)}
+ORDER_D = (3, 1, 2, 0)
 
 B_QUERY, B_VALUE, B_OUT, FIRST_GAIN, FIRST_SHIFT, B_DOWN, SECOND_GAIN, SECOND_SHIFT, B_UP = range(9)
 
 ROWS = 256
+TILE = 256
 PART = 128
 WIDTH = 768
 STEP = 128
@@ -325,13 +327,13 @@
     tokens_in, lengths_in, cot_in, w_qkv_in, w_out_in, w_up_in, w_down_in,
     b_query_in, b_value_in, b_out_in, first_gain_in, first_shift_in, b_up_in, b_down_in, second_gain_in, second_shift_in,
     tokens_out, grad_out, down_out, up_out, qkv_out, vec_out,
-    w_qkv, w_out, w_up, w_down, par, tok, cot, q3, k3, v3, bias, probs, hidden, xhat, rstd, low, slope, wide, total,
+    w_qkv, w_out, w_up, w_down, par, tok, cot, q3, k3, v3, bias, probs, hidden, xhat, rstd, low, slope, wide, total, held, turned, inverse, d_scores,
     dsum, dctx3, dkv_own, dkv_send, dkv_in, dq_t, dqkv_flat, out_rows, grad_rows,
     act, dpre, dffn_t, hid_t, tok_t, ctx_t, dqkv, dbr,
-    sums_0, sums_1, sums_2, in1_0, in1_1, in1_2, in2_0, in2_1, in2_2, in3_0, in3_1, in3_2,
+    sums_0, sums_1, sums_2, sums_z, in1_0, in1_1, in1_2, in2_0, in2_1, in2_2, in3_0, in3_1, in3_2, in1_z, in2_z, in3_z,
     vec_mine, vec_in,
     load, ex_send, ex_recv, core_send, core_recv, act_send, act_recv,
-    send1, recv1, send2, recv2, send3, recv3, vec_send, vec_recv, vec_load,
+    send1, recv1, send2, recv2, send3, recv3, send_z, recv_z, vec_send, vec_recv, vec_load,
     held_0, held_1, held_2, held_3, held_4, held_5, held_6, held_7, held_8,
 ):
     z, y, x, core = place()
@@ -339,7 +341,9 @@
     at_core = device(z, y, x, 1 - core)
     at_x = device(z, y, 1 - x, core)
     at_y = device(z, 1 - y, x, core)
-    at_z = [device((z + k) % 4, y, x, core) for k in (1, 2, 3)]
+    at_place = [z, z + 1 - 2 * (z % 2), (z + 2) % 4, 3 - z]
+    at_z1 = device(at_place[1], y, x, core)
+    at_z2 = device(at_place[2], y, x, core)
 
     loads = [pltpu.make_async_copy(tokens_in.at[x], tok.at[pl.ds(0, PART)], load.at[0])]
     for n, s in enumerate((1, 2, 0)):
@@ -363,15 +367,15 @@
         SECOND_SHIFT: (second_shift_in, held_7), B_UP: (b_up_in, held_8),
     }
     vec_loads = [
-        pltpu.make_async_copy(source, held, vec_load.at[n]) for n, (source, held) in enumerate(vec_refs.values())
+        pltpu.make_async_copy(source, vector, vec_load.at[n]) for n, (source, vector) in enumerate(vec_refs.values())
     ]
     for copy in vec_loads:
         copy.start()
 
     barrier = pltpu.get_barrier_semaphore()
-    for where in [at_core, at_x, at_y] + at_z:
+    for where in (at_core, at_x, at_y, at_z1, at_z2):
         pl.semaphore_signal(barrier, inc=1, device_id=where, device_id_type=MESH_ID)
-    pl.semaphore_wait(barrier, 6)
+    pl.semaphore_wait(barrier, 5)
 
     get_tok = remote(tokens_in.at[1 - x], tok.at[pl.ds(PART, PART)], ex_send.at[0], ex_recv.at[0], at_x)
     get_cot = remote(cot_in.at[1 - x], cot.at[pl.ds(PART, PART)], ex_send.at[1], ex_recv.at[1], at_x)
@@ -388,12 +392,12 @@
 
     for copy in vec_loads:
         copy.wait()
-    for row, (_, held) in vec_refs.items():
+    for row, (_, vector) in vec_refs.items():
         if row == B_UP:
             for t in range(4):
-                par[B_UP + t : B_UP + t + 1, :] = held[WIDTH * t : WIDTH * (t + 1)].reshape(1, WIDTH)
+                par[B_UP + t : B_UP + t + 1, :] = vector[WIDTH * t : WIDTH * (t + 1)].reshape(1, WIDTH)
         else:
-            par[row : row + 1, :] = held[...].reshape(1, WIDTH)
+            par[row : row + 1, :] = vector[...].reshape(1, WIDTH)
     vec_mine[0] = jnp.zeros((16, WIDTH), F32)
     length = lengths_in[0, x]
     mine, across = 2 * x + core, 2 * (1 - x) + core
@@ -416,6 +420,8 @@
         else:
             get_tok.wait_recv()
             get_cot.start()
+            for copy in loads[4:14]:
+                copy.start()
         for n, s in enumerate((1, 2, 0)):
             if b == 0:
                 loads[1 + n].wait()
@@ -427,18 +433,13 @@
             part = part.astype(BF16)
             if s == 0:
                 part = part * jnp.asarray(0.125, BF16)
-            held = (q3, k3, v3)[s]
+            heads = (q3, k3, v3)[s]
             for j in range(6):
-                held[j, rows, :] = part[:, 128 * j : 128 * (j + 1)]
+                heads[j, rows, :] = part[:, 128 * j : 128 * (j + 1)]
             if s:
                 kv_copies.append(
-                    to_core(held.at[:, pl.ds(PART * b, PART)], held.at[:, pl.ds(ROWS + PART * b, PART)])
+                    to_core(heads.at[:, pl.ds(PART * b, PART)], heads.at[:, pl.ds(ROWS + PART * b, PART)])
                 )
-        if b == 0:
-            for copy in loads[5:14]:
-                copy.start()
-        else:
-            loads[4].start()
     tok_t[:, 0:ROWS] = tok[...].T
     qkv_copies = [to_core(tok_t.at[:, pl.ds(0, ROWS)], tok_t.at[:, pl.ds(ROWS, ROWS)])]
     for copy in kv_copies:
@@ -450,18 +451,41 @@
         zeros = jnp.zeros_like(pair)
         return jnp.where(low_half, pair, zeros) if h == 0 else jnp.where(low_half, zeros, pair)
 
-    def attend(j, _):
-        queries, keys = q3[j], k3[j]
-        values_t = v3[j].T
-        for h in range(2):
-            scores = dot_t(keys, half_of(queries, h)) + bias[...]
-            exponent = jnp.exp(scores - jnp.max(scores, axis=0, keepdims=True))
-            weight = (exponent * (1.0 / jnp.sum(exponent, axis=0, keepdims=True))).astype(BF16)
-            probs[2 * j + h] = weight
-            ctx_t[pl.ds(pl.multiple_of(128 * j + 64 * h, 64), 64), 0:ROWS] = dot(values_t[64 * h : 64 * (h + 1)], weight).astype(BF16)
-        return 0
-
-    lax.fori_loop(0, 6, attend, 0, unroll=True)
+    for j in range(6):
+        turned[j] = v3[j].T
+    highest = {}
+
+    def score(n):
+        queries = half_of(q3[n // 2], n % 2)
+        top = None
+        for t in range(0, 512, TILE):
+            scores = dot_t(k3[n // 2, t : t + TILE], queries) + bias[t : t + TILE, :]
+            held[n % 2, t : t + TILE, :] = scores
+            part = jnp.max(scores.reshape(TILE // 8, 8, ROWS), axis=0)
+            top = part if top is None else jnp.maximum(top, part)
+        highest[n] = jnp.max(top, axis=0, keepdims=True)
+
+    def weigh(n):
+        sums = None
+        for t in range(0, 512, TILE):
+            exponent = jnp.exp(held[n % 2, t : t + TILE, :] - highest[n])
+            part = fold(exponent)
+            sums = part if sums is None else sums + part
+            probs[n, t : t + TILE, :] = exponent.astype(BF16)
+        inverse[n : n + 1, :] = 1.0 / jnp.sum(sums, axis=0, keepdims=True)
+
+    def gather(n):
+        context = dot(turned[n // 2, 64 * (n % 2) : 64 * (n % 2 + 1)], probs[n]) * inverse[n : n + 1, :]
+        ctx_t[64 * n : 64 * (n + 1), 0:ROWS] = context.astype(BF16)
+
+    score(0)
+    for n in range(12):
+        if n < 11:
+            score(n + 1)
+        weigh(n)
+        if n:
+            gather(n - 1)
+    gather(11)
     qkv_copies.append(to_core(ctx_t.at[:, pl.ds(0, ROWS)], ctx_t.at[:, pl.ds(ROWS, ROWS)]))
 
     loads[5].wait()
@@ -543,23 +567,24 @@
         down_copies.append(to_core(dffn_t.at[there, :, pl.ds(0, ROWS)], dffn_t.at[there, :, pl.ds(ROWS, ROWS)]))
 
     def first(m, k):
-        zk = (z + k) % 4
+        zk = at_place[k]
         if (m, k) in X_FIRST:
             return remote(sums[m].at[1 - x, zk], in1[m].at[zk], send1.at[m, k], recv1.at[m, k], at_x)
         return remote(sums[m].at[:, zk, 1 - y], in1[m].at[zk], send1.at[m, k], recv1.at[m, k], at_y)
 
     def second(m, k):
-        zk = (z + k) % 4
+        zk = at_place[k]
         if (m, k) in X_FIRST:
             return remote(sums[m].at[x, zk, 1 - y], in2[m].at[zk], send2.at[m, k], recv2.at[m, k], at_y)
         return remote(sums[m].at[1 - x, zk, y], in2[m].at[zk], send2.at[m, k], recv2.at[m, k], at_x)
 
     def third(m, k):
-        zk = (z + k) % 4
-        return remote(sums[m].at[x, zk, y], in3[m].at[k - 1], send3.at[m, k], recv3.at[m, k], at_z[k - 1])
+        zk = at_place[k]
+        slot, where = ((0, at_z1), (2, at_z2), (1, at_z1))[k - 1]
+        return remote(sums[m].at[x, zk, y], in3[m].at[slot], send3.at[m, k], recv3.at[m, k], where)
 
     def add_first(m, k):
-        zk = (z + k) % 4
+        zk = at_place[k]
         if (m, k) in X_FIRST:
             sums[m][x, zk] = sums[m][x, zk] + in1[m][zk]
         else:
@@ -567,11 +592,45 @@
                 sums[m][b, zk, y] = sums[m][b, zk, y] + in1[m][zk, b]
 
     def add_second(m, k):
-        zk = (z + k) % 4
-        sums[m][x, zk, y] = sums[m][x, zk, y] + in2[m][zk]
+        zk = at_place[k]
+        block = sums[m][x, zk, y] + in2[m][zk]
+        if k == 2:
+            third(m, 3).wait_recv()
+            block = block + in3[m][1]
+        sums[m][x, zk, y] = block
+
+    z_near = [
+        remote(sums_z.at[:, at_place[k]], in1_z.at[n], send_z.at[n], recv_z.at[n], at_z1) for n, k in enumerate((1, 3))
+    ]
+    z_far = remote(sums_z.at[:, at_place[2]], in1_z.at[2], send_z.at[2], recv_z.at[2], at_z2)
+    z_second = remote(sums_z.at[1 - x, z], in2_z, send_z.at[3], recv_z.at[3], at_x)
+    z_third = remote(sums_z.at[x, z, 1 - y], in3_z, send_z.at[4], recv_z.at[4], at_y)
+
+    def at_z_first(step):
+        if step == 1:
+            z_near[1].wait_recv()
+            for b in range(2):
+                sums_z[b, at_place[2]] = sums_z[b, at_place[2]] + in1_z[1, b]
+            z_far.start()
+        elif step == 2:
+            z_near[0].wait_recv()
+            z_far.wait_recv()
+            for b in range(2):
+                sums_z[b, z] = (sums_z[b, z].astype(F32) + in1_z[0, b].astype(F32) + in1_z[2, b].astype(F32)).astype(BF16)
+            z_second.start()
+        elif step == 3:
+            z_second.wait_recv()
+            sums_z[x, z] = sums_z[x, z] + in2_z[...]
+            z_third.start()
+        else:
+            z_third.wait_recv()
+            down_out[96:192, :] = sums_z[x, z, y].astype(F32) + in3_z[...].astype(F32)
 
     def at(point):
         for step, m, k in PLAN[point]:
+            if m == DOWN_Z:
+                at_z_first(step)
+                continue
             if step == 0:
                 first(m, k).start()
             elif step == 1:
@@ -603,11 +662,14 @@
         copy.wait_recv()
     left = jnp.concatenate([dffn_t[core], dffn_t[2 + core]], axis=0)
     for k in ORDER_D:
-        t = (z + k) % 4
+        t = at_place[k]
         part = dot(left, act[t]).astype(BF16)
         for b in range(2):
             for h in range(2):
-                sums_0[b, t, h] = part[192 * b : 192 * (b + 1), 384 * h : 384 * (h + 1)]
+                sums_0[b, t, h] = part[192 * b : 192 * b + 96, 384 * h : 384 * (h + 1)]
+                sums_z[b, t, h] = part[192 * b + 96 : 192 * (b + 1), 384 * h : 384 * (h + 1)]
+        if k % 2:
+            z_near[k // 2].start()
         if (0, DOWN, k) in PLAN[0]:
             first(DOWN, k).start()
     for n, j in enumerate((0, 2)):
@@ -647,31 +709,52 @@
 
     at(4)
 
-    def attend_back(j, _):
-        queries, keys, values, d_ctx = q3[j], k3[j], v3[j], dctx3[j]
-        keys_t = keys.T
-        d_keys = jnp.zeros((512, 128), F32)
-        d_values = jnp.zeros((512, 128), F32)
-        for h in range(2):
-            d_head = half_of(d_ctx, h)
-            weight = probs[2 * j + h]
-            d_probs = dot_t(values, d_head)
-            d_values = d_values + dot(weight, d_head)
-            wide_weight = weight.astype(F32)
-            inner = jnp.sum(wide_weight * d_probs, axis=0, keepdims=True)
-            d_scores = (wide_weight * (d_probs - inner)).astype(BF16)
-            d_keys = d_keys + dot(d_scores, half_of(queries, h))
-            dq_t[pl.ds(pl.multiple_of(128 * j + 64 * h, 64), 64), :] = (dot(keys_t[64 * h : 64 * (h + 1)], d_scores) * 0.125).astype(BF16)
-        dkv_own[0, j] = d_keys[0:ROWS]
-        dkv_own[1, j] = d_values[0:ROWS]
-        dkv_send[0, j] = d_keys[ROWS:].astype(BF16)
-        dkv_send[1, j] = d_values[ROWS:].astype(BF16)
-        return 0
-
-    lax.fori_loop(0, 3, attend_back, 0, unroll=True)
+    for j in range(6):
+        turned[j] = k3[j].T
+    inverse_t = inverse[...].T
+    inner, d_heads, partial_values, partial_keys = {}, {}, {}, {}
+
+    def probs_back(n):
+        d_head = (half_of(dctx3[n // 2], n % 2).astype(F32) * inverse_t[:, n : n + 1]).astype(BF16)
+        sums = None
+        for t in range(0, 512, TILE):
+            d_probs = dot_t(v3[n // 2, t : t + TILE], d_head)
+            held[n % 2, t : t + TILE, :] = d_probs
+            part = fold(probs[n, t : t + TILE, :].astype(F32) * d_probs)
+            sums = part if sums is None else sums + part
+        inner[n] = jnp.sum(sums, axis=0, keepdims=True) * inverse[n : n + 1, :]
+        partial_values[n] = dot(probs[n], d_head)
+
+    def scores_back(n):
+        for t in range(0, 512, TILE):
+            d = probs[n, t : t + TILE, :].astype(F32) * (held[n % 2, t : t + TILE, :] - inner[n])
+            d_scores[n % 2, t : t + TILE, :] = d.astype(BF16)
+
+    def keys_back(n):
+        j, h = n // 2, n % 2
+        d_queries = dot(turned[j, 64 * h : 64 * (h + 1)], d_scores[h]) * 0.125
+        dq_t[64 * n : 64 * (n + 1), :] = d_queries.astype(BF16)
+        partial_keys[n] = dot(d_scores[h], half_of(q3[j], h))
+        if h:
+            for s, partial in enumerate((partial_keys, partial_values)):
+                total_pair = partial[n - 1] + partial[n]
+                dkv_own[s, j] = total_pair[0:ROWS]
+                dkv_send[s, j] = total_pair[ROWS:].astype(BF16)
+
+    def attend_back(start, stop):
+        probs_back(start)
+        for n in range(start, stop):
+            if n < stop - 1:
+                probs_back(n + 1)
+            scores_back(n)
+            if n > start:
+                keys_back(n - 1)
+        keys_back(stop - 1)
+
+    attend_back(0, 6)
     back_copies = [to_core(dkv_send.at[:, pl.ds(0, 3)], dkv_in.at[:, pl.ds(0, 3)])]
     at(5)
-    lax.fori_loop(3, 6, attend_back, 0, unroll=True)
+    attend_back(6, 12)
     back_copies.append(to_core(dkv_send.at[:, pl.ds(3, 3)], dkv_in.at[:, pl.ds(3, 3)]))
     at(6)
     d_queries = dq_t[...].T
@@ -695,7 +778,8 @@
         there = j + 1 - core
         qkv_copies.append(to_core(dqkv.at[there, pl.ds(0, ROWS)], dqkv.at[there, pl.ds(ROWS, ROWS)]))
     vec_steps = [
-        remote(vec_mine.at[s], vec_in.at[s], vec_send.at[s], vec_recv.at[s], w) for s, w in enumerate((at_core, at_x, at_y))
+        remote(vec_mine.at[s], vec_in.at[s], vec_send.at[s], vec_recv.at[s], w)
+        for s, w in enumerate((at_core, at_x, at_y, at_z1, at_z2))
     ]
     vec_steps[0].start()
     at(9)
@@ -725,33 +809,30 @@
     at(13)
     vec_steps[2].wait_recv()
     vec_mine[3] = vec_mine[2] + vec_in[2]
-    vec_z = [
-        remote(vec_mine.at[3], vec_in.at[3 + z], vec_send.at[2 + k], vec_recv.at[2 + k], at_z[k - 1])
-        for k in (1, 2, 3)
-    ]
-    for copy in vec_z:
-        copy.start()
-    vec_in[3 + z] = vec_mine[3]
+    vec_steps[3].start()
     at(14)
-    for copy in vec_z:
-        copy.wait_recv()
-    vec_out[...] = (vec_in[3] + vec_in[4]) + (vec_in[5] + vec_in[6])
+    vec_steps[3].wait_recv()
+    vec_mine[4] = vec_mine[3] + vec_in[3]
+    vec_steps[4].start()
+    at(15)
+    vec_steps[4].wait_recv()
+    vec_out[...] = vec_mine[4] + vec_in[4]
     for m, out in ((DOWN, down_out), (UP, up_out), (QKV, qkv_out)):
-        for k in (1, 2, 3):
-            third(m, k).wait_recv()
-        block = sums[m][x, z, y].astype(F32)
-        for k in range(3):
-            block = block + in3[m][k].astype(F32)
-        out[...] = block
+        third(m, 1).wait_recv()
+        third(m, 2).wait_recv()
+        block = sums[m][x, z, y].astype(F32) + in3[m][0].astype(F32) + in3[m][2].astype(F32)
+        out[0 : BLOCKS[m][0], :] = block
 
     out_across.wait_recv()
     grad_across.wait_recv()
     out_local.wait()
     grad_local.wait()
-    for copy in [get_tok, get_cot, out_across, grad_across] + core_copies + vec_steps + vec_z:
+    for copy in [get_tok, get_cot, out_across, grad_across] + core_copies + vec_steps:
         copy.wait_send()
     for t in range(4):
         act_copy(t).wait_send()
+    for copy in z_near + [z_far, z_second, z_third]:
+        copy.wait_send()
     for m in (DOWN, UP, QKV):
         for k in range(4):
             first(m, k).wait_send()
@@ -808,26 +889,28 @@
         B((6, ROWS, 128), BF16), B((6, 512, 128), BF16), B((6, 512, 128), BF16),
         B((512, ROWS), F32), B((12, 512, ROWS), BF16),
         B((ROWS, W), F32), B((ROWS, W), F32), B((ROWS, 1), F32), B((ROWS, W), BF16),
-        B((4, ROWS, W), F32), B((ROWS, W), F32), B((ROWS, W), F32), B((ROWS, W), F32),
+        B((4, ROWS, W), F32), B((ROWS, W), F32), B((ROWS, W), F32),
+        B((2, 512, ROWS), F32), B((6, 128, 512), BF16), B((16, ROWS), F32), B((2, 512, ROWS), BF16), B((ROWS, W), F32),
         B((6, ROWS, 128), BF16), B((2, 6, ROWS, 128), F32), B((2, 6, ROWS, 128), BF16), B((2, 6, ROWS, 128), BF16),
         B((W, ROWS), BF16), B((ROWS, 3 * W), BF16), B((ROWS, W), BF16), B((ROWS, W), BF16),
         B((4, 512, W), BF16), B((4, 512, W), BF16), B((4, 192, 512), BF16),
         B((W, 512), BF16), B((W, 512), BF16), B((W, 512), BF16), B((4, 512, 640), BF16), B((4, 512, 256), BF16),
     ]
     scratch += [B((2, 4, 2) + block, BF16) for block in BLOCKS]
-    scratch += [B((4, 2) + block, BF16) for block in BLOCKS]
-    scratch += [B((4,) + block, BF16) for block in BLOCKS]
-    scratch += [B((3,) + block, BF16) for block in BLOCKS]
-    scratch += [B((4, 16, W), F32), B((7, 16, W), F32)]
+    scratch += [B((4, 2) + block, BF16) for block in BLOCKS[:DOWN_Z]]
+    scratch += [B((4,) + block, BF16) for block in BLOCKS[:DOWN_Z]]
+    scratch += [B((3,) + block, BF16) for block in BLOCKS[:DOWN_Z]]
+    scratch += [B((3, 2, 2) + BLOCKS[DOWN_Z], BF16), B((2,) + BLOCKS[DOWN_Z], BF16), B(BLOCKS[DOWN_Z], BF16)]
+    scratch += [B((5, 16, W), F32), B((5, 16, W), F32)]
     scratch += [dma((16,)), dma((4,)), dma((4,)), dma((24,)), dma((24,)), dma((4,)), dma((4,))]
-    scratch += [dma((3, 4))] * 6 + [dma((6,)), dma((6,)), dma((9,))] + [B((W,), F32)] * 8 + [B((4 * W,), F32)]
+    scratch += [dma((3, 4))] * 6 + [dma((5,)), dma((5,)), dma((5,)), dma((5,)), dma((9,))] + [B((W,), F32)] * 8 + [B((4 * W,), F32)]
     results = pl.pallas_call(
         layer_kernel,
         name="layer",
         out_shape=(
             jax.ShapeDtypeStruct(tokens.shape, BF16),
             jax.ShapeDtypeStruct(tokens.shape, BF16),
-            jax.ShapeDtypeStruct(BLOCKS[DOWN], F32),
+            jax.ShapeDtypeStruct((192, 384), F32),
             jax.ShapeDtypeStruct(BLOCKS[UP], F32),
             jax.ShapeDtypeStruct(BLOCKS[QKV], F32),
             jax.ShapeDtypeStruct((16, W), F32),

time: 108 us -> 94.1 us (0.87)
  Pallas kernels: 106 us -> 93 us
    pallas_call x1, Pallas kernels: 104 us -> 90.4 us  [local(): pl.pallas_call(layer_kernel, name='layer', out_shape=(jax.ShapeDtypeStruc...]
where the time goes in v4:
time: 94.1 us; the launch traced here: 93.9 us
  Pallas kernels  93 us (99%)
    pallas_call x1, Pallas kernels, local(): pl.pallas_call(layer_kernel, name='layer', out_shape=(jax.ShapeDtypeStruc...  90.4 us
    pallas_call x1, Pallas kernels, finish(): pl.pallas_call(finish_kernel, name='finish', out_shape=tuple((jax.ShapeDt...  2.63 us

profile of v4, /device:TPU:0, one launch (start us, length us, event | category | flops | bytes accessed | tf_op | source)
XLA Modules:
  0.0 93.9 jit_solution(11463713830633879153)
XLA Ops:
  0.7 90.4 %layer.1 = (bf16[2,128,768]{2,1,0:T(8,128)(2,1)}, bf16[2,128,768]{2,1,0:T(8,128)(2,1)}, f32[192,384]{1,0:T(8,128)}, f32[96,768]{1,0:T(8,128)}, f32[96,768]{1,0:T(8,128)}, /*index=5*/f32[16,768]{1,0:T(8,128)}) custom-call(bf16[2,128,768]{2,1,0:T(8,128)(2,1)} %tokens_in.1, s32[1,2]{1,0:T(1,128)} %lengths_in.1, bf16[2,128,768]{2,1,0:T(8,128)(2,1)} %cot_in.1, ...), custom_call_target="tpu_custom_call" | custom-call | tf_op jit(solution)/shard_map/layer/pallas_call | solution.py:907
  91.1 2.6 %finish.1 = (bf16[2,128,768]{2,1,0:T(8,128)(2,1)}, bf16[2,128,768]{2,1,0:T(8,128)(2,1)}, f32[96,576]{1,0:T(8,128)}, f32[96,192]{1,0:T(8,128)}, f32[96,768]{1,0:T...) custom-call(bf16[2,128,768]{2,1,0:T(8,128)(2,1)} %get-tuple-element., ...), custom_call_target="tpu_custom_call" | custom-call | tf_op jit(solution)/shard_map/finish/pallas_call | solution.py:868

commit v5 on v4

--- a/solution.py
+++ b/solution.py
@@ -256,27 +256,29 @@
 
 
 DOWN, UP, QKV, DOWN_Z = 0, 1, 2, 3
-BLOCKS = ((96, 384), (96, 768), (96, 768), (96, 384))
+SPLIT = 64
+BLOCKS = ((SPLIT, 384), (96, 768), (96, 768), (192 - SPLIT, 384))
 PLAN = (
-    ((0, 0, 3), (0, 0, 1), (0, 0, 2),),
+    ((0, 0, 3), (0, 0, 2), (0, 0, 1), (0, 0, 0),),
     (),
-    ((0, 0, 0),),
-    ((0, 1, 3),),
-    ((0, 1, 1), (0, 1, 2),),
-    ((1, 0, 3), (1, 0, 1), (1, 3, 0),),
-    ((1, 0, 2),),
     (),
-    ((1, 0, 0), (1, 1, 3),),
+    ((0, 1, 3), (0, 1, 2),),
+    ((0, 1, 1), (0, 1, 0), (1, 0, 3), (1, 0, 0), (1, 0, 2),),
+    ((1, 0, 1),),
+    ((1, 3, 0),),
+    ((1, 1, 2),),
     (),
-    ((0, 1, 0),),
-    ((0, 2, 3),),
-    ((1, 1, 1), (1, 1, 2), (2, 0, 1), (2, 0, 3), (2, 3, 0),),
-    ((2, 1, 3), (2, 0, 0),),
-    ((2, 0, 2), (0, 2, 1), (1, 1, 0),),
-    ((1, 2, 3), (2, 1, 2), (1, 2, 1), (0, 2, 2), (2, 1, 1), (2, 2, 3), (0, 2, 0), (3, 3, 0), (2, 1, 0), (1, 2, 2), (2, 2, 1), (2, 2, 2), (1, 2, 0), (4, 3, 0), (2, 2, 0),),
+    (),
+    ((1, 1, 3),),
+    ((0, 2, 3), (0, 2, 2), (1, 1, 0), (2, 0, 3),),
+    ((1, 1, 1), (2, 0, 1), (2, 0, 0),),
+    ((2, 1, 3), (2, 3, 0),),
+    ((0, 2, 1), (2, 0, 2), (1, 2, 2),),
+    ((1, 2, 3), (2, 1, 2), (2, 1, 1), (2, 1, 0), (0, 2, 0), (5, 1, 0), (3, 3, 0), (1, 2, 1), (2, 2, 3), (5, 0, 0), (2, 2, 2), (2, 2, 1), (1, 2, 0), (4, 3, 0),),
+    ((2, 2, 0),),
 )
-X_FIRST = {(0, 1), (1, 2), (1, 3), (2, 3)}
-ORDER_D = (3, 1, 2, 0)
+X_FIRST = {(0, 0), (1, 0), (1, 2), (2, 2)}
+ORDER_D = (3, 2, 1, 0)
 
 B_QUERY, B_VALUE, B_OUT, FIRST_GAIN, FIRST_SHIFT, B_DOWN, SECOND_GAIN, SECOND_SHIFT, B_UP = range(9)
 
@@ -326,12 +328,12 @@
 def layer_kernel(
     tokens_in, lengths_in, cot_in, w_qkv_in, w_out_in, w_up_in, w_down_in,
     b_query_in, b_value_in, b_out_in, first_gain_in, first_shift_in, b_up_in, b_down_in, second_gain_in, second_shift_in,
-    tokens_out, grad_out, down_out, up_out, qkv_out, vec_out,
-    w_qkv, w_out, w_up, w_down, par, tok, cot, q3, k3, v3, bias, probs, hidden, xhat, rstd, low, slope, wide, total, held, turned, inverse, d_scores,
+    tokens_out, grad_out, down_hbm, up_hbm, qkv_hbm, vec_hbm,
+    w_qkv, w_out, w_up, w_down, par, tok, cot, q3, k3, v3, bias, probs, hidden, xhat, rstd, low, d_ffn, slope, wide, total, held, turned, inverse, d_scores,
     dsum, dctx3, dkv_own, dkv_send, dkv_in, dq_t, dqkv_flat, out_rows, grad_rows,
     act, dpre, dffn_t, hid_t, tok_t, ctx_t, dqkv, dbr,
     sums_0, sums_1, sums_2, sums_z, in1_0, in1_1, in1_2, in2_0, in2_1, in2_2, in3_0, in3_1, in3_2, in1_z, in2_z, in3_z,
-    vec_mine, vec_in,
+    vec_mine, vec_in, down_out, up_out, qkv_out, vec_out,
     load, ex_send, ex_recv, core_send, core_recv, act_send, act_recv,
     send1, recv1, send2, recv2, send3, recv3, send_z, recv_z, vec_send, vec_recv, vec_load,
     held_0, held_1, held_2, held_3, held_4, held_5, held_6, held_7, held_8,
@@ -505,12 +507,10 @@
         return 0
 
     lax.fori_loop(0, ROWS // STEP, first_norm, 0)
-    hid_t[:, 0:ROWS] = low[...].T
-    up_copies = [to_core(hid_t.at[:, pl.ds(0, ROWS)], hid_t.at[:, pl.ds(ROWS, ROWS)])]
+    up_copies = []
 
     for n in range(6, 14):
         loads[n].wait()
-    total[...] = jnp.zeros_like(total)
 
     def act_copy(t):
         return remote(act.at[t, pl.ds(0, ROWS)], act.at[t, pl.ds(ROWS, ROWS)], act_send.at[t], act_recv.at[t], at_core)
@@ -522,43 +522,48 @@
         act[t, 0:ROWS, :] = active
         slope[t] = phi + u * jnp.exp(-0.5 * u * u) * INV_ROOT_TWO_PI
         act_copy(t).start()
-        total[...] += dot(active, w_down[t])
+        product = dot(active, w_down[t])
+        total[...] = total[...] + product if t else product
 
     loads[4].wait()
     get_cot.wait_recv()
 
-    def second_norm(r, carry):
+    def live_rows(r):
+        n = lax.broadcasted_iota(jnp.int32, (STEP, 1), 0) + STEP * r
+        return jnp.where(jnp.where(n < PART, mine * PART + n, across * PART + n - PART) < length, 1.0, 0.0)
+
+    def second_norm(r, _):
         rows = pl.ds(pl.multiple_of(STEP * r, STEP), STEP)
         value = hidden[rows, :] + (total[rows, :] + par[B_DOWN : B_DOWN + 1, :])
         center = value - mean(value)
         root = lax.rsqrt(mean(center * center) + EPSILON)
         normed = center * root
-        n = lax.broadcasted_iota(jnp.int32, (STEP, 1), 0) + STEP * r
-        live = jnp.where(jnp.where(n < PART, mine * PART + n, across * PART + n - PART) < length, 1.0, 0.0)
+        wide[rows, :] = normed
+        e = cot[rows, :].astype(F32) * live_rows(r) * par[SECOND_GAIN : SECOND_GAIN + 1, :]
+        d = root * (e - mean(e) - normed * mean(e * normed))
+        dsum[rows, :] = d
+        d_ffn[rows, :] = d.astype(BF16)
+        return 0
+
+    lax.fori_loop(0, ROWS // STEP, second_norm, 0)
+
+    def second_norm_rest(r, carry):
+        rows = pl.ds(pl.multiple_of(STEP * r, STEP), STEP)
+        live, normed = live_rows(r), wide[rows, :]
         out = (normed * par[SECOND_GAIN : SECOND_GAIN + 1, :] + par[SECOND_SHIFT : SECOND_SHIFT + 1, :]) * live
         out_rows[rows, :] = out.astype(BF16)
         grad = cot[rows, :].astype(F32) * live
-        e = grad * par[SECOND_GAIN : SECOND_GAIN + 1, :]
-        d = root * (e - mean(e) - normed * mean(e * normed))
-        dsum[rows, :] = d
-        d_low = d.astype(BF16)
-        low[rows, :] = d_low
         gain, shift, down = carry
-        return gain + fold(grad * normed), shift + fold(grad), down + fold(d_low.astype(F32))
+        return gain + fold(grad * normed), shift + fold(grad), down + fold(d_ffn[rows, :].astype(F32))
 
     zero = jnp.zeros((8, WIDTH), F32)
-    gain, shift, down = lax.fori_loop(0, ROWS // STEP, second_norm, (zero, zero, zero))
 
     def put(row, partial):
         vec_mine[0, row : row + 1, :] = jnp.sum(partial, axis=0, keepdims=True)
 
-    put(SECOND_GAIN, gain)
-    put(SECOND_SHIFT, shift)
-    put(B_DOWN, down)
     out_local = pltpu.make_async_copy(out_rows.at[pl.ds(0, PART)], tokens_out.at[x], load.at[14])
     out_across = remote(out_rows.at[pl.ds(PART, PART)], tokens_out.at[x], ex_send.at[2], ex_recv.at[2], at_x)
-    out_local.start()
-    dffn_all = low[...].T
+    dffn_all = d_ffn[...].T
     for j in range(4):
         dffn_t[j, :, 0:ROWS] = dffn_all[192 * j : 192 * (j + 1), :]
     down_copies = []
@@ -624,10 +629,13 @@
             z_third.start()
         else:
             z_third.wait_recv()
-            down_out[96:192, :] = sums_z[x, z, y].astype(F32) + in3_z[...].astype(F32)
+            down_out[SPLIT:192, :] = sums_z[x, z, y].astype(F32) + in3_z[...].astype(F32)
 
     def at(point):
         for step, m, k in PLAN[point]:
+            if step == 5:
+                (out_across, grad_across)[m].start()
+                continue
             if m == DOWN_Z:
                 at_z_first(step)
                 continue
@@ -643,13 +651,14 @@
                 if k:
                     third(m, k).start()
 
-    total[...] = dsum[...]
+    before = [dsum]
 
     def feed_back(t):
-        d_pre = (dot_t(low[...], w_down[t]) * slope[t]).astype(BF16)
+        d_pre = (dot_t(d_ffn[...], w_down[t]) * slope[t]).astype(BF16)
         dpre[t, 0:ROWS, :] = d_pre
         vec_mine[0, pl.ds(B_UP + t, 1), :] = jnp.sum(fold(d_pre.astype(F32)), axis=0, keepdims=True)
-        total[...] += dot_t(d_pre, w_up[t])
+        total[...] = before[-1][...] + dot_t(d_pre, w_up[t])
+        before.append(total)
 
     for j in (0, 2):
         there = j + 1 - core
@@ -666,12 +675,14 @@
         part = dot(left, act[t]).astype(BF16)
         for b in range(2):
             for h in range(2):
-                sums_0[b, t, h] = part[192 * b : 192 * b + 96, 384 * h : 384 * (h + 1)]
-                sums_z[b, t, h] = part[192 * b + 96 : 192 * (b + 1), 384 * h : 384 * (h + 1)]
+                sums_0[b, t, h] = part[192 * b : 192 * b + SPLIT, 384 * h : 384 * (h + 1)]
+                sums_z[b, t, h] = part[192 * b + SPLIT : 192 * (b + 1), 384 * h : 384 * (h + 1)]
         if k % 2:
             z_near[k // 2].start()
         if (0, DOWN, k) in PLAN[0]:
             first(DOWN, k).start()
+    hid_t[:, 0:ROWS] = low[...].T
+    up_copies.append(to_core(hid_t.at[:, pl.ds(0, ROWS)], hid_t.at[:, pl.ds(ROWS, ROWS)]))
     for n, j in enumerate((0, 2)):
         feed_back(j + core)
         at(1 + n)
@@ -682,6 +693,11 @@
             part = dot(hid_t[...], dpre[2 * b + core, :, 256 * n : 256 * (n + 1)]).astype(BF16)
             sums_1[b, :, :, :, 256 * n : 256 * (n + 1)] = part.reshape(4, 2, 96, 256)
     at(3)
+    gain, shift, down = lax.fori_loop(0, ROWS // STEP, second_norm_rest, (zero, zero, zero))
+    put(SECOND_GAIN, gain)
+    put(SECOND_SHIFT, shift)
+    put(B_DOWN, down)
+    out_local.start()
 
     def first_norm_back(r, carry):
         rows = pl.ds(pl.multiple_of(STEP * r, STEP), STEP)
@@ -800,8 +816,6 @@
     grad_local = pltpu.make_async_copy(grad_rows.at[pl.ds(0, PART)], grad_out.at[x], load.at[15])
     grad_across = remote(grad_rows.at[pl.ds(PART, PART)], grad_out.at[x], ex_send.at[3], ex_recv.at[3], at_x)
     grad_local.start()
-    grad_across.start()
-    out_across.start()
     at(12)
     vec_steps[1].wait_recv()
     vec_mine[2] = vec_mine[1] + vec_in[1]
@@ -817,16 +831,29 @@
     at(15)
     vec_steps[4].wait_recv()
     vec_out[...] = vec_mine[4] + vec_in[4]
-    for m, out in ((DOWN, down_out), (UP, up_out), (QKV, qkv_out)):
+    results = [pltpu.make_async_copy(vec_out, vec_hbm, load.at[19])]
+    results[0].start()
+
+    def finish_block(m):
+        out, target = ((down_out, down_hbm), (up_out, up_hbm), (qkv_out, qkv_hbm))[m]
         third(m, 1).wait_recv()
         third(m, 2).wait_recv()
         block = sums[m][x, z, y].astype(F32) + in3[m][0].astype(F32) + in3[m][2].astype(F32)
         out[0 : BLOCKS[m][0], :] = block
+        results.append(pltpu.make_async_copy(out, target, load.at[16 + m]))
+        results[-1].start()
+
+    finish_block(DOWN)
+    finish_block(UP)
+    at(16)
+    finish_block(QKV)
 
     out_across.wait_recv()
     grad_across.wait_recv()
     out_local.wait()
     grad_local.wait()
+    for copy in results:
+        copy.wait()
     for copy in [get_tok, get_cot, out_across, grad_across] + core_copies + vec_steps:
         copy.wait_send()
     for t in range(4):
@@ -845,33 +872,56 @@
     tokens_in, grad_in, down_in, up_in, joined_in, vec_in,
     tokens_out, grad_out, qkv_out, out_out, up_out, down_out,
     b_query, b_value, b_out, first_gain, first_shift, b_up, b_down, second_gain, second_shift,
+    tokens, grad, down, up, joined, vec, qkv, out, vec_0, vec_1, vec_2, vec_3, vec_4, vec_5, vec_6, vec_7, vec_8, get, give,
 ):
-    tokens_out[...] = tokens_in[...]
-    grad_out[...] = grad_in[...]
-    up_out[...] = up_in[...]
-    qkv_out[...] = joined_in[:, 0:576]
-    out_out[...] = joined_in[:, 576:WIDTH]
-    down_out[...] = down_in[...]
-    for row, ref in (
-        (B_QUERY, b_query), (B_VALUE, b_value), (B_OUT, b_out), (FIRST_GAIN, first_gain), (FIRST_SHIFT, first_shift),
-        (B_DOWN, b_down), (SECOND_GAIN, second_gain), (SECOND_SHIFT, second_shift),
+    pairs = ((joined_in, joined), (vec_in, vec), (tokens_in, tokens), (grad_in, grad), (down_in, down), (up_in, up))
+    gets = [pltpu.make_async_copy(source, held, get.at[n]) for n, (source, held) in enumerate(pairs)]
+    for copy in gets:
+        copy.start()
+    gives = []
+
+    def put(held, target):
+        gives.append(pltpu.make_async_copy(held, target, give.at[len(gives)]))
+        gives[-1].start()
+
+    for n, (held, target) in ((2, (tokens, tokens_out)), (3, (grad, grad_out)), (4, (down, down_out)), (5, (up, up_out))):
+        gets[n].wait()
+        put(held, target)
+    gets[0].wait()
+    qkv[...] = joined[:, 0:576]
+    put(qkv, qkv_out)
+    out[...] = joined[:, 576:WIDTH]
+    put(out, out_out)
+    gets[1].wait()
+    for row, held, target in (
+        (B_QUERY, vec_0, b_query), (B_VALUE, vec_1, b_value), (B_OUT, vec_2, b_out), (FIRST_GAIN, vec_3, first_gain),
+        (FIRST_SHIFT, vec_4, first_shift), (B_DOWN, vec_5, b_down), (SECOND_GAIN, vec_6, second_gain),
+        (SECOND_SHIFT, vec_7, second_shift),
     ):
-        ref[...] = vec_in[row, :]
+        held[...] = vec[row, :]
+        put(held, target)
     for t in range(4):
-        b_up[WIDTH * t : WIDTH * (t + 1)] = vec_in[B_UP + t, :]
+        vec_8[WIDTH * t : WIDTH * (t + 1)] = vec[B_UP + t, :]
+    put(vec_8, b_up)
+    for copy in gives:
+        copy.wait()
 
 
 def finish(out_tokens, grad_tokens, down, up, joined, vectors):
-    vmem = pl.BlockSpec(memory_space=pltpu.VMEM)
+    hbm = pl.BlockSpec(memory_space=pl.ANY)
     W = WIDTH
     shapes = [out_tokens.shape] * 2 + [(96, 576), (96, 192), up.shape, down.shape] + [(W,)] * 5 + [(4 * W,)] + [(W,)] * 3
+    inputs = (out_tokens, grad_tokens, down, up, joined, vectors)
+    scratch = [pltpu.VMEM(a.shape, a.dtype) for a in inputs] + [pltpu.VMEM((96, 576), F32), pltpu.VMEM((96, 192), F32)]
+    scratch += [pltpu.VMEM((W,), F32)] * 8 + [pltpu.VMEM((4 * W,), F32)]
     outs = pl.pallas_call(
         finish_kernel,
         name="finish",
         out_shape=tuple(jax.ShapeDtypeStruct(s, BF16 if n < 2 else F32) for n, s in enumerate(shapes)),
-        in_specs=[vmem] * 6,
-        out_specs=(vmem,) * 15,
-    )(out_tokens, grad_tokens, down, up, joined, vectors)
+        in_specs=[hbm] * 6,
+        out_specs=(hbm,) * 15,
+        scratch_shapes=scratch + [pltpu.SemaphoreType.DMA((6,)), pltpu.SemaphoreType.DMA((15,))],
+    )(*inputs)
     return outs[:5] + (outs[5].T,) + outs[6:]
 
 
@@ -879,7 +929,6 @@
     tokens, lengths, cotangent, w_qkv, b_query, b_value, w_out, b_out, first_gain, first_shift, w_up, b_up, w_down, b_down,
     second_gain, second_shift,
 ):
-    vmem = pl.BlockSpec(memory_space=pltpu.VMEM)
     hbm = pl.BlockSpec(memory_space=pl.ANY)
     dma = pltpu.SemaphoreType.DMA
     B, W = pltpu.VMEM, WIDTH
@@ -888,7 +937,7 @@
         B((ROWS, W), BF16), B((ROWS, W), BF16),
         B((6, ROWS, 128), BF16), B((6, 512, 128), BF16), B((6, 512, 128), BF16),
         B((512, ROWS), F32), B((12, 512, ROWS), BF16),
-        B((ROWS, W), F32), B((ROWS, W), F32), B((ROWS, 1), F32), B((ROWS, W), BF16),
+        B((ROWS, W), F32), B((ROWS, W), F32), B((ROWS, 1), F32), B((ROWS, W), BF16), B((ROWS, W), BF16),
         B((4, ROWS, W), F32), B((ROWS, W), F32), B((ROWS, W), F32),
         B((2, 512, ROWS), F32), B((6, 128, 512), BF16), B((16, ROWS), F32), B((2, 512, ROWS), BF16), B((ROWS, W), F32),
         B((6, ROWS, 128), BF16), B((2, 6, ROWS, 128), F32), B((2, 6, ROWS, 128), BF16), B((2, 6, ROWS, 128), BF16),
@@ -902,7 +951,8 @@
     scratch += [B((3,) + block, BF16) for block in BLOCKS[:DOWN_Z]]
     scratch += [B((3, 2, 2) + BLOCKS[DOWN_Z], BF16), B((2,) + BLOCKS[DOWN_Z], BF16), B(BLOCKS[DOWN_Z], BF16)]
     scratch += [B((5, 16, W), F32), B((5, 16, W), F32)]
-    scratch += [dma((16,)), dma((4,)), dma((4,)), dma((24,)), dma((24,)), dma((4,)), dma((4,))]
+    scratch += [B((192, 384), F32), B(BLOCKS[UP], F32), B(BLOCKS[QKV], F32), B((16, W), F32)]
+    scratch += [dma((20,)), dma((4,)), dma((4,)), dma((24,)), dma((24,)), dma((4,)), dma((4,))]
     scratch += [dma((3, 4))] * 6 + [dma((5,)), dma((5,)), dma((5,)), dma((5,)), dma((9,))] + [B((W,), F32)] * 8 + [B((4 * W,), F32)]
     results = pl.pallas_call(
         layer_kernel,
@@ -916,7 +966,7 @@
             jax.ShapeDtypeStruct((16, W), F32),
         ),
         in_specs=[hbm, pl.BlockSpec(memory_space=pltpu.SMEM)] + [hbm] * 14,
-        out_specs=(hbm, hbm) + (vmem,) * 4,
+        out_specs=(hbm,) * 6,
         scratch_shapes=scratch,
         compiler_params=pltpu.CompilerParams(
             collective_id=1, has_side_effects=True, vmem_limit_bytes=63 * 1024 * 1024

time: 94.1 us -> 89.8 us (0.954)
  Pallas kernels: 93 us -> 88.8 us
    pallas_call x1, Pallas kernels: 90.4 us -> 86.3 us  [local(): pl.pallas_call(layer_kernel, name='layer', out_shape=(jax.ShapeDtypeStruc...]
where the time goes in v5:
time: 89.8 us; the launch traced here: 89.6 us
  Pallas kernels  88.8 us (99%)
    pallas_call x1, Pallas kernels, local(): pl.pallas_call(layer_kernel, name='layer', out_shape=(jax.ShapeDtypeStruc...  86.3 us
    pallas_call x1, Pallas kernels, finish(): pl.pallas_call(finish_kernel, name='finish', out_shape=tuple((jax.ShapeDt...  2.5 us

profile of v5, /device:TPU:0, one launch (start us, length us, event | category | flops | bytes accessed | tf_op | source)
XLA Modules:
  0.0 89.6 jit_solution(14890934536983966123)
XLA Ops:
  0.7 86.3 %layer.1 = (bf16[2,128,768]{2,1,0:T(8,128)(2,1)}, bf16[2,128,768]{2,1,0:T(8,128)(2,1)}, f32[192,384]{1,0:T(8,128)}, f32[96,768]{1,0:T(8,128)}, f32[96,768]{1,0:T(8,128)}, /*index=5*/f32[16,768]{1,0:T(8,128)}) custom-call(bf16[2,128,768]{2,1,0:T(8,128)(2,1)} %tokens_in.1, s32[1,2]{1,0:T(1,128)} %lengths_in.1, bf16[2,128,768]{2,1,0:T(8,128)(2,1)} %cot_in.1, ...), custom_call_target="tpu_custom_call" | custom-call | tf_op jit(solution)/shard_map/layer/pallas_call | solution.py:957
  86.9 2.5 %finish.1 = (bf16[2,128,768]{2,1,0:T(8,128)(2,1)}, bf16[2,128,768]{2,1,0:T(8,128)(2,1)}, f32[96,576]{1,0:T(8,128)}, f32[96,192]{1,0:T(8,128)}, f32[96,768]{1,0:T...) custom-call(bf16[2,128,768]{2,1,0:T(8,128)(2,1)} %get-tuple-element., ...), custom_call_target="tpu_custom_call" | custom-call | tf_op jit(solution)/shard_map/finish/pallas_call | solution.py:917

commit v6 on v5

--- a/solution.py
+++ b/solution.py
@@ -256,7 +256,7 @@
 
 
 DOWN, UP, QKV, DOWN_Z = 0, 1, 2, 3
-SPLIT = 64
+SPLIT = 48
 BLOCKS = ((SPLIT, 384), (96, 768), (96, 768), (192 - SPLIT, 384))
 PLAN = (
     ((0, 0, 3), (0, 0, 2), (0, 0, 1), (0, 0, 0),),
@@ -274,10 +274,10 @@
     ((1, 1, 1), (2, 0, 1), (2, 0, 0),),
     ((2, 1, 3), (2, 3, 0),),
     ((0, 2, 1), (2, 0, 2), (1, 2, 2),),
-    ((1, 2, 3), (2, 1, 2), (2, 1, 1), (2, 1, 0), (0, 2, 0), (5, 1, 0), (3, 3, 0), (1, 2, 1), (2, 2, 3), (5, 0, 0), (2, 2, 2), (2, 2, 1), (1, 2, 0), (4, 3, 0),),
+    ((1, 2, 3), (0, 2, 0), (2, 1, 2), (2, 1, 1), (2, 1, 0), (5, 1, 0), (3, 3, 0), (1, 2, 1), (2, 2, 3), (5, 0, 0), (2, 2, 2), (2, 2, 1), (1, 2, 0), (4, 3, 0),),
     ((2, 2, 0),),
 )
-X_FIRST = {(0, 0), (1, 0), (1, 2), (2, 2)}
+X_FIRST = {(0, 0), (0, 1), (1, 0), (1, 2), (2, 2)}
 ORDER_D = (3, 2, 1, 0)
 
 B_QUERY, B_VALUE, B_OUT, FIRST_GAIN, FIRST_SHIFT, B_DOWN, SECOND_GAIN, SECOND_SHIFT, B_UP = range(9)

time: 89.8 us -> 88.1 us (0.981)
  Pallas kernels: 88.8 us -> 87.1 us
    pallas_call x1, Pallas kernels: 86.3 us -> 84.6 us  [local(): pl.pallas_call(layer_kernel, name='layer', out_shape=(jax.ShapeDtypeStruc...]
where the time goes in v6:
time: 88.1 us; the launch traced here: 87.9 us
  Pallas kernels  87.1 us (99%)
    pallas_call x1, Pallas kernels, local(): pl.pallas_call(layer_kernel, name='layer', out_shape=(jax.ShapeDtypeStruc...  84.6 us
    pallas_call x1, Pallas kernels, finish(): pl.pallas_call(finish_kernel, name='finish', out_shape=tuple((jax.ShapeDt...  2.5 us

profile of v6, /device:TPU:0, one launch (start us, length us, event | category | flops | bytes accessed | tf_op | source)
XLA Modules:
  0.0 87.9 jit_solution(2958719594005100683)
XLA Ops:
  0.7 84.6 %layer.1 = (bf16[2,128,768]{2,1,0:T(8,128)(2,1)}, bf16[2,128,768]{2,1,0:T(8,128)(2,1)}, f32[192,384]{1,0:T(8,128)}, f32[96,768]{1,0:T(8,128)}, f32[96,768]{1,0:T(8,128)}, /*index=5*/f32[16,768]{1,0:T(8,128)}) custom-call(bf16[2,128,768]{2,1,0:T(8,128)(2,1)} %tokens_in.1, s32[1,2]{1,0:T(1,128)} %lengths_in.1, bf16[2,128,768]{2,1,0:T(8,128)(2,1)} %cot_in.1, ...), custom_call_target="tpu_custom_call" | custom-call | tf_op jit(solution)/shard_map/layer/pallas_call | solution.py:957
  85.2 2.5 %finish.1 = (bf16[2,128,768]{2,1,0:T(8,128)(2,1)}, bf16[2,128,768]{2,1,0:T(8,128)(2,1)}, f32[96,576]{1,0:T(8,128)}, f32[96,192]{1,0:T(8,128)}, f32[96,768]{1,0:T...) custom-call(bf16[2,128,768]{2,1,0:T(8,128)(2,1)} %get-tuple-element., ...), custom_call_target="tpu_custom_call" | custom-call | tf_op jit(solution)/shard_map/finish/pallas_call | solution.py:917

commit v7 on v6

--- a/solution.py
+++ b/solution.py
@@ -491,11 +491,11 @@
     qkv_copies.append(to_core(ctx_t.at[:, pl.ds(0, ROWS)], ctx_t.at[:, pl.ds(ROWS, ROWS)]))
 
     loads[5].wait()
-    wide[...] = dot(ctx_t[:, 0:ROWS].T, w_out[...])
-
-    def first_norm(r, _):
-        rows = pl.ds(pl.multiple_of(STEP * r, STEP), STEP)
-        value = tok[rows, :].astype(F32) + wide[rows, :] + par[B_OUT : B_OUT + 1, :]
+
+    def first_norm(r):
+        rows = pl.ds(STEP * r, STEP)
+        branch = dot(ctx_t[:, STEP * r : STEP * (r + 1)].T, w_out[...]) + par[B_OUT : B_OUT + 1, :]
+        value = tok[rows, :].astype(F32) + branch
         center = value - mean(value)
         root = lax.rsqrt(mean(center * center) + EPSILON)
         normed = center * root
@@ -506,7 +506,8 @@
         low[rows, :] = out.astype(BF16)
         return 0
 
-    lax.fori_loop(0, ROWS // STEP, first_norm, 0)
+    for r in range(ROWS // STEP):
+        first_norm(r)
     up_copies = []
 
     for n in range(6, 14):
@@ -532,8 +533,8 @@
         n = lax.broadcasted_iota(jnp.int32, (STEP, 1), 0) + STEP * r
         return jnp.where(jnp.where(n < PART, mine * PART + n, across * PART + n - PART) < length, 1.0, 0.0)
 
-    def second_norm(r, _):
-        rows = pl.ds(pl.multiple_of(STEP * r, STEP), STEP)
+    def second_norm(r):
+        rows = pl.ds(STEP * r, STEP)
         value = hidden[rows, :] + (total[rows, :] + par[B_DOWN : B_DOWN + 1, :])
         center = value - mean(value)
         root = lax.rsqrt(mean(center * center) + EPSILON)
@@ -545,7 +546,8 @@
         d_ffn[rows, :] = d.astype(BF16)
         return 0
 
-    lax.fori_loop(0, ROWS // STEP, second_norm, 0)
+    for r in range(ROWS // STEP):
+        second_norm(r)
 
     def second_norm_rest(r, carry):
         rows = pl.ds(pl.multiple_of(STEP * r, STEP), STEP)

time: 88.1 us -> 88.2 us (level)
  no operation moved by 1% of the time
where the time goes in v7:
time: 88.2 us; the launch traced here: 87.9 us
  Pallas kernels  87.1 us (99%)
    pallas_call x1, Pallas kernels, local(): pl.pallas_call(layer_kernel, name='layer', out_shape=(jax.ShapeDtypeStruc...  84.6 us
    pallas_call x1, Pallas kernels, finish(): pl.pallas_call(finish_kernel, name='finish', out_shape=tuple((jax.ShapeDt...  2.5 us

profile of v7, /device:TPU:0, one launch (start us, length us, event | category | flops | bytes accessed | tf_op | source)
XLA Modules:
  0.0 87.9 jit_solution(9964067391776383134)
XLA Ops:
  0.7 84.6 %layer.1 = (bf16[2,128,768]{2,1,0:T(8,128)(2,1)}, bf16[2,128,768]{2,1,0:T(8,128)(2,1)}, f32[192,384]{1,0:T(8,128)}, f32[96,768]{1,0:T(8,128)}, f32[96,768]{1,0:T(8,128)}, /*index=5*/f32[16,768]{1,0:T(8,128)}) custom-call(bf16[2,128,768]{2,1,0:T(8,128)(2,1)} %tokens_in.1, s32[1,2]{1,0:T(1,128)} %lengths_in.1, bf16[2,128,768]{2,1,0:T(8,128)(2,1)} %cot_in.1, ...), custom_call_target="tpu_custom_call" | custom-call | tf_op jit(solution)/shard_map/layer/pallas_call | solution.py:959
  85.3 2.5 %finish.1 = (bf16[2,128,768]{2,1,0:T(8,128)(2,1)}, bf16[2,128,768]{2,1,0:T(8,128)(2,1)}, f32[96,576]{1,0:T(8,128)}, f32[96,192]{1,0:T(8,128)}, f32[96,768]{1,0:T...) custom-call(bf16[2,128,768]{2,1,0:T(8,128)(2,1)} %get-tuple-element., ...), custom_call_target="tpu_custom_call" | custom-call | tf_op jit(solution)/shard_map/finish/pallas_call | solution.py:919
